TPU v7x, 256 devices: a whole 4x4x8 slice. The times are simulated.
256 devices in a mesh: dp: 8 (over z_hi, core), ctx: 32 (over x, z_lo, y).
Axes of the slice: x: 4, y: 4, z: 8 (z_hi: 4, z_lo: 2; z = z_hi * 2 + z_lo), core: 2. Of those that a mesh axis runs over, the one named last changes fastest.
Arguments:
- query_proj: bfloat16 [8, 4096, 1024], P('dp', 'ctx'), may hold values from -6 to 6
- key_proj: bfloat16 [8, 4096, 1024], P('dp', 'ctx'), may hold values from -6 to 6
- value_proj: bfloat16 [8, 4096, 1024], P('dp', 'ctx'), may hold values from -6 to 6
- out_grad: bfloat16 [8, 4096, 1024], P('dp', 'ctx'), may hold values from -6 to 6
- filter_taps: float32 [4096, 1024], P(None, 'ctx'), may hold values from -0.09375 to 0.09375
Outputs:
- query_grad: bfloat16 [8, 4096, 1024], P('dp', 'ctx')
- key_grad: bfloat16 [8, 4096, 1024], P('dp', 'ctx')
- value_grad: bfloat16 [8, 4096, 1024], P('dp', 'ctx')
- taps_grad: float32 [4096, 1024], P('dp', 'ctx')
All inputs are finite; a program needn't handle non-finite values.
Results may differ from a plain program's by a relative error of at most 0.0058.
Values may be sent and summed in bfloat16 or wider, within the bound.
A program may use at most 64 MiB of HBM per device.

v0:
```python
import math

import jax
import jax.numpy as jnp
from jax import lax
from jax.sharding import PartitionSpec as P

HIGHEST = lax.Precision.HIGHEST


def split_length(points):
    outer_len = math.gcd(points, 2 ** (points.bit_length() // 2))
    return (outer_len, points // outer_len)


def phase_table(row_count, col_count, modulus):
    row_index = lax.broadcasted_iota(jnp.int32, (row_count, col_count), 0)
    col_index = lax.broadcasted_iota(jnp.int32, (row_count, col_count), 1)
    phase = 2.0 * math.pi / modulus * (row_index * col_index % modulus).astype(jnp.float32)
    return (jnp.cos(phase), -jnp.sin(phase))


def middle_mix(block, table):
    return jnp.einsum("bjc,jk->bkc", block, table, precision=HIGHEST)


def forward_real(signal, outer_len, inner_len):
    channels = signal.shape[1]
    inner_re, inner_im = phase_table(inner_len, inner_len, inner_len)
    folded = signal.reshape(inner_len, outer_len * channels)
    section_re = jnp.dot(inner_re, folded, precision=HIGHEST).reshape(
        inner_len, outer_len, channels
    )
    section_im = jnp.dot(inner_im, folded, precision=HIGHEST).reshape(
        inner_len, outer_len, channels
    )
    twist_re, twist_im = phase_table(inner_len, outer_len, inner_len * outer_len)
    twist_re = twist_re[:, :, None]
    twist_im = twist_im[:, :, None]
    turned_re = section_re * twist_re - section_im * twist_im
    turned_im = section_re * twist_im + section_im * twist_re
    outer_re, outer_im = phase_table(outer_len, outer_len, outer_len)
    spec_re = middle_mix(turned_re, outer_re) - middle_mix(turned_im, outer_im)
    spec_im = middle_mix(turned_re, outer_im) + middle_mix(turned_im, outer_re)
    return (spec_re, spec_im)


def inverse_real(spec_re, spec_im, outer_len, inner_len):
    channels = spec_re.shape[2]
    outer_re, outer_im = phase_table(outer_len, outer_len, outer_len)
    back_re = middle_mix(spec_re, outer_re) + middle_mix(spec_im, outer_im)
    back_im = middle_mix(spec_im, outer_re) - middle_mix(spec_re, outer_im)
    twist_re, twist_im = phase_table(inner_len, outer_len, inner_len * outer_len)
    twist_re = twist_re[:, :, None]
    twist_im = twist_im[:, :, None]
    turned_re = back_re * twist_re + back_im * twist_im
    turned_im = back_im * twist_re - back_re * twist_im
    inner_re, inner_im = phase_table(inner_len, inner_len, inner_len)
    folded_re = turned_re.reshape(inner_len, outer_len * channels)
    folded_im = turned_im.reshape(inner_len, outer_len * channels)
    signal = jnp.dot(inner_re, folded_re, precision=HIGHEST) + jnp.dot(
        inner_im, folded_im, precision=HIGHEST
    )
    return signal.reshape(inner_len * outer_len, channels) / (inner_len * outer_len)


def gated(first, second):
    return (first.astype(jnp.float32) * second.astype(jnp.float32)).astype(jnp.bfloat16)


def on_device(query_proj, key_proj, value_proj, out_grad, filter_taps):
    length = query_proj.shape[1] * lax.axis_size("ctx")
    outer_len, inner_len = split_length(2 * length)
    kernel_re, kernel_im = forward_real(
        jnp.pad(filter_taps, ((0, length), (0, 0))), outer_len, inner_len
    )

    def per_sequence(mixed_row, product_row):
        product_pad = jnp.pad(product_row.astype(jnp.float32), ((0, length), (0, 0)))
        mixed_pad = jnp.pad(mixed_row.astype(jnp.float32), ((0, length), (0, 0)))
        product_re, product_im = forward_real(product_pad, outer_len, inner_len)
        mixed_re, mixed_im = forward_real(mixed_pad, outer_len, inner_len)
        convolved = inverse_real(
            kernel_re * product_re - kernel_im * product_im,
            kernel_re * product_im + kernel_im * product_re,
            outer_len,
            inner_len,
        )[:length]
        inner_part = inverse_real(
            mixed_re * kernel_re + mixed_im * kernel_im,
            mixed_im * kernel_re - mixed_re * kernel_im,
            outer_len,
            inner_len,
        )[:length]
        kernel_part = inverse_real(
            mixed_re * product_re + mixed_im * product_im,
            mixed_im * product_re - mixed_re * product_im,
            outer_len,
            inner_len,
        )[:length]
        return (convolved.astype(jnp.bfloat16), inner_part.astype(jnp.bfloat16), kernel_part)

    query_cols, key_cols, value_cols, grad_cols = (
        lax.all_to_all(query_proj, "ctx", split_axis=2, concat_axis=1, tiled=True),
        lax.all_to_all(key_proj, "ctx", split_axis=2, concat_axis=1, tiled=True),
        lax.all_to_all(value_proj, "ctx", split_axis=2, concat_axis=1, tiled=True),
        lax.all_to_all(out_grad, "ctx", split_axis=2, concat_axis=1, tiled=True),
    )
    product_cols = gated(key_cols, value_cols)
    mixed_cols = gated(grad_cols, query_cols)
    convolved, inner_grad, kernel_parts = jax.vmap(per_sequence)(mixed_cols, product_cols)
    kernel_grad = jnp.sum(kernel_parts, axis=0)
    norm_scale = 1.0 / math.sqrt(query_proj.shape[0] * lax.axis_size("dp") * length)
    taps_grad = lax.psum_scatter(kernel_grad * norm_scale, "dp", scatter_dimension=0, tiled=True)
    query_back = gated(grad_cols, convolved)
    key_cols_grad = gated(inner_grad, value_cols)
    value_cols_grad = gated(inner_grad, key_cols)
    query_grad, key_grad, value_grad = (
        lax.all_to_all(query_back, "ctx", split_axis=1, concat_axis=2, tiled=True),
        lax.all_to_all(key_cols_grad, "ctx", split_axis=1, concat_axis=2, tiled=True),
        lax.all_to_all(value_cols_grad, "ctx", split_axis=1, concat_axis=2, tiled=True),
    )
    return (query_grad, key_grad, value_grad, taps_grad)


def solution(mesh):
    placed = (
        P("dp", "ctx", None),
        P("dp", "ctx", None),
        P("dp", "ctx", None),
        P("dp", "ctx", None),
        P(None, "ctx"),
    )
    return jax.shard_map(
        on_device,
        mesh=mesh,
        in_specs=placed,
        out_specs=(
            P("dp", "ctx", None),
            P("dp", "ctx", None),
            P("dp", "ctx", None),
            P("dp", "ctx"),
        ),
        check_vma=False,
    )
```

profile of v0, /device:TPU:2, one launch (start us, length us, event | category | flops | bytes accessed | tf_op | source)
XLA Modules:
  0.0 341.4 jit_solution(12419155267592050507)
XLA Ops:
  9.0 2.2 reduce.1
  12.0 9.4 %all-to-all-start.1 = ((bf16[32,2,2048]{2,1,0:T(2,128)(2,1)}), bf16[32,2,2048]{2,1,0:T(2,128)(2,1)S(1)}, u32[]{:S(2)}, u32[]{:S(2)}) async-start(bf16[32,2,2048]{2,1,0:T(2,128)(2,1)} %reshape.427), calls=%async_computation.1 | async-start | bytes 524288 | tf_op jit(solution)/shard_map/all_to_all | solution.py:105
  22.2 2.2 pad.13.clone
  24.4 3.5 %reshape.398 = f32[64,4096]{1,0:T(8,128)S(1)} reshape(f32[8192,32]{1,0:T(8,128)} %pad.13.clone) | data formatting | bytes 2097152 | tf_op jit(solution)/shard_map/reshape | solution.py:30
  33.4 2.2 reduce.2
  36.4 2.2 fusion.40
  39.9 9.1 %all-to-all-start.2 = ((bf16[32,2,2048]{2,1,0:T(2,128)(2,1)}), bf16[32,2,2048]{2,1,0:T(2,128)(2,1)}, u32[]{:S(2)}, u32[]{:S(2)}) async-start(bf16[32,2,2048]{2,1,0:T(2,128)(2,1)} %reshape.429), calls=%async_computation.2 | async-start | bytes 524288 | tf_op jit(solution)/shard_map/all_to_all | solution.py:106
  49.0 3.5 %fusion.17 = f32[1,64,128,32]{2,1,3,0:T(8,128)} fusion(f32[128,64,32]{0,1,2:T(8,128)} %fusion.40, f32[64,128,32]{1,0,2:T(8,128)S(1)} %fusion.85, f32[64,128,32]{1,0,2:T(8,128)S(1)} %fusion.91, f32[64,128]{1,0:T(8,128)S(1)} %get-tuple-element.50, f32[64,128]{1,0:T(8,128)S(1)} %get-tuple-element.51), kind=kOutput, calls=%fused_computation.33 | convolution fusion | flops 403947520 | bytes 4259840 | tf_op jit(solution)/shard_map/bjc,jk->bkc/dot_general | solution.py:24
  54.4 3.8 %reduce = bf16[1024,128]{1,0:T(8,128)(2,1)} reduce(bf16[1024,1,128]{2,1,0:T(2,128)(2,1)} %bitcast.266, bf16[]{:T(256)} %broadcast.443), dimensions={1}, to_apply=%bitcast.203.reduce_sub_computation | reduce | bytes 524290
  61.9 3.8 %reduce.3 = bf16[1024,128]{1,0:T(8,128)(2,1)} reduce(bf16[1024,1,128]{2,1,0:T(2,128)(2,1)} %bitcast.267, bf16[]{:T(256)} %broadcast.443), dimensions={1}, to_apply=%bitcast.211.reduce_sub_computation | reduce | bytes 524290
  67.4 2.2 fusion.15
  70.3 8.6 %all-to-all-start = ((bf16[32,2,2048]{2,1,0:T(2,128)(2,1)}), bf16[32,2,2048]{2,1,0:T(2,128)(2,1)S(1)}, u32[]{:S(2)}, u32[]{:S(2)}) async-start(bf16[32,2,2048]{2,1,0:T(2,128)(2,1)} %reshape.425), calls=%async_computation | async-start | bytes 524288 | tf_op jit(solution)/shard_map/all_to_all | solution.py:107
  78.9 2.2 reshape.430
  85.9 2.3 reshape.399
  91.1 8.4 %all-to-all-start.4 = ((bf16[32,2,2048]{2,1,0:T(2,128)(2,1)}), bf16[32,2,2048]{2,1,0:T(2,128)(2,1)}, u32[]{:S(2)}, u32[]{:S(2)}) async-start(bf16[32,2,2048]{2,1,0:T(2,128)(2,1)} %reshape.433), calls=%async_computation.4 | async-start | bytes 524288 | tf_op jit(solution)/shard_map/all_to_all | solution.py:104
  100.5 2.2 fusion.42
  102.7 2.2 fusion.41
  104.9 2.6 all-to-all-done.4
  107.5 2.8 reshape.434
  113.2 2.3 copy.257
  115.4 2.9 pad.15.clone
  118.3 3.9 %reshape.404 = bf16[64,4096]{1,0:T(8,128)(2,1)S(1)} reshape(bf16[1,8192,32]{2,1,0:T(8,128)(2,1)} %pad.15.clone) | data formatting | bytes 1048576 | tf_op jit(solution)/shard_map/reshape.360
  123.6 2.2 copy.234
  149.6 4.0 %multiply_subtract_fusion = (f32[1,64,128,32]{2,1,3,0:T(8,128)}, f32[1,64,128,32]{2,1,3,0:T(8,128)}, f32[1,64,128,32]{2,1,3,0:T(8,128)}, f32[1,64,128,32]{2,1,3,...) fusion(f32[1,64,128,32]{2,1,3,0:T(8,128)S(1)} %fusion.6, f32[64,128]{1,0:T(8,128)S(1)} %get-tuple-element.50, ...), kind=kOutput, calls=%fused_computation.52 | convolution fusion | flops 407879680 | bytes 13697024 | tf_op jit(solution)/shard_map/vmap(bjc,jk->bkc)/dot_general | solution.py:24
  153.6 3.1 copy.247
  156.7 3.5 %fusion.120 = f32[64,4096]{1,0:T(8,128)} fusion(f32[64,4096]{0,1:T(8,128)S(1)} %bitcast.239), kind=kOutput, calls=%fused_computation.159 | convolution fusion | flops 201383936 | bytes 2097152 | tf_op jit(solution)/shard_map/vmap()/dot_general | solution.py:61
  160.2 3.1 copy.248
  163.2 4.7 %fusion = f32[64,4096]{1,0:T(8,128)} fusion(f32[64,4096]{1,0:T(8,128)} %fusion.120, f32[64,4096]{0,1:T(8,128)S(1)} %bitcast.244), kind=kOutput, calls=%fused_computation.1 | convolution fusion | flops 201912320 | bytes 3145728 | tf_op jit(solution)/shard_map/vmap()/dot_general | solution.py:61
  167.9 4.1 %div.20 = f32[1,8192,32]{2,1,0:T(8,128)} reshape(f32[64,4096]{1,0:T(8,128)} %fusion) | data formatting | bytes 2097152 | tf_op jit(solution)/shard_map/vmap()/div | solution.py:64
  172.1 3.1 fusion.5
  175.2 3.1 copy.236
  178.2 3.5 %fusion.116 = f32[64,4096]{1,0:T(8,128)} fusion(f32[64,4096]{0,1:T(8,128)S(1)} %bitcast.240), kind=kOutput, calls=%fused_computation.157 | convolution fusion | flops 201383936 | bytes 2097152 | tf_op jit(solution)/shard_map/vmap()/dot_general | solution.py:61
  181.7 3.1 copy.237
  184.8 4.6 %fusion.4 = bf16[64,4096]{1,0:T(8,128)(2,1)} fusion(f32[64,4096]{1,0:T(8,128)} %fusion.116, f32[64,4096]{0,1:T(8,128)S(1)} %bitcast.236), kind=kOutput, calls=%fused_computation.7 | convolution fusion | flops 202174464 | bytes 2621440 | tf_op jit(solution)/shard_map/vmap()/dot_general | solution.py:61
  189.4 2.5 div.18
  195.2 2.8 copy.244
  198.0 22.6 %reduce.6 = bf16[4096,32]{1,0:T(8,128)(2,1)S(1)} reduce(bf16[4096,1,32]{2,1,0:T(2,128)(2,1)S(1)} %bitcast.246, bf16[]{:T(256)} %broadcast.443), dimensions={1}, to_apply=%bitcast.215.reduce_sub_computation | reduce | bytes 524290
  222.3 6.1 %all-to-all-start.6 = ((bf16[32,2,2048]{2,1,0:T(2,128)(2,1)}), bf16[32,2,2048]{2,1,0:T(2,128)(2,1)}, u32[]{:S(2)}, u32[]{:S(2)}) async-start(bf16[32,2,2048]{2,1,0:T(2,128)(2,1)} %reshape.437), calls=%async_computation.6 | async-start | bytes 524288 | tf_op jit(solution)/shard_map/all_to_all | solution.py:121
  228.4 2.8 copy.240
  231.1 22.7 %reduce.5 = bf16[4096,32]{1,0:T(8,128)(2,1)S(1)} reduce(bf16[4096,1,32]{2,1,0:T(2,128)(2,1)S(1)} %bitcast.247, bf16[]{:T(256)} %broadcast.443), dimensions={1}, to_apply=%bitcast.213.reduce_sub_computation | reduce | bytes 524290
  255.5 4.2 %copy.222 = f32[1,64,128,32]{1,3,2,0:T(8,128)} copy(f32[1,64,128,32]{2,1,3,0:T(8,128)} %get-tuple-element.46) | data formatting | bytes 2097152 | tf_op jit(solution)/shard_map/vmap()/add | solution.py:56
  261.5 4.1 %fusion.118 = f32[64,4096]{1,0:T(8,128)S(1)} fusion(f32[64,4096]{0,1:T(8,128)} %bitcast.237), kind=kOutput, calls=%fused_computation.158 | convolution fusion | flops 201383936 | bytes 2097152 | tf_op jit(solution)/shard_map/vmap()/dot_general | solution.py:61
  265.6 2.5 fusion.3
  272.4 8.7 %all-to-all-start.5 = ((bf16[32,2,2048]{2,1,0:T(2,128)(2,1)}), bf16[32,2,2048]{2,1,0:T(2,128)(2,1)S(1)}, u32[]{:S(2)}, u32[]{:S(2)}) async-start(bf16[32,2,2048]{2,1,0:T(2,128)(2,1)} %reshape.435), calls=%async_computation.5 | async-start | bytes 524288 | tf_op jit(solution)/shard_map/all_to_all | solution.py:120
  281.4 2.8 copy.226
  284.2 22.4 %reduce.4 = bf16[4096,32]{1,0:T(8,128)(2,1)S(1)} reduce(bf16[4096,1,32]{2,1,0:T(2,128)(2,1)S(1)} %bitcast.245, bf16[]{:T(256)} %broadcast.443), dimensions={1}, to_apply=%bitcast.209.reduce_sub_computation | reduce | bytes 524290
  308.3 8.3 %all-to-all-start.3 = ((bf16[32,2,2048]{2,1,0:T(2,128)(2,1)}), bf16[32,2,2048]{2,1,0:T(2,128)(2,1)S(1)}, u32[]{:S(2)}, u32[]{:S(2)}) async-start(bf16[32,2,2048]{2,1,0:T(2,128)(2,1)} %reshape.431), calls=%async_computation.3 | async-start | bytes 524288 | tf_op jit(solution)/shard_map/all_to_all | solution.py:119
  316.6 3.9 %reshape.438 = bf16[4096,1,32]{2,1,0:T(2,128)(2,1)S(1)} reshape(bf16[32,2,2048]{2,1,0:T(2,128)(2,1)} %all-to-all-done.6) | data formatting | bytes 524288
  (113 shorter events, 83.6 us)
Async XLA Ops:
  7.2 14.4 %copy-start.9 = (f32[4096,32]{0,1:T(8,128)S(1)}, f32[4096,32]{0,1:T(8,128)}, u32[]{:S(2)}) copy-start(f32[4096,32]{0,1:T(8,128)} %param.9) | copy-start | bytes 1572868
  12.0 27.8 %all-to-all-start.1 = ((bf16[32,2,2048]{2,1,0:T(2,128)(2,1)}), bf16[32,2,2048]{2,1,0:T(2,128)(2,1)S(1)}, u32[]{:S(2)}, u32[]{:S(2)}) async-start(bf16[32,2,2048]{2,1,0:T(2,128)(2,1)} %reshape.427), calls=%async_computation.1 | async-start | bytes 524288 | tf_op jit(solution)/shard_map/all_to_all | solution.py:105
  39.9 30.5 %all-to-all-start.2 = ((bf16[32,2,2048]{2,1,0:T(2,128)(2,1)}), bf16[32,2,2048]{2,1,0:T(2,128)(2,1)}, u32[]{:S(2)}, u32[]{:S(2)}) async-start(bf16[32,2,2048]{2,1,0:T(2,128)(2,1)} %reshape.429), calls=%async_computation.2 | async-start | bytes 524288 | tf_op jit(solution)/shard_map/all_to_all | solution.py:106
  70.3 20.8 %all-to-all-start = ((bf16[32,2,2048]{2,1,0:T(2,128)(2,1)}), bf16[32,2,2048]{2,1,0:T(2,128)(2,1)S(1)}, u32[]{:S(2)}, u32[]{:S(2)}) async-start(bf16[32,2,2048]{2,1,0:T(2,128)(2,1)} %reshape.425), calls=%async_computation | async-start | bytes 524288 | tf_op jit(solution)/shard_map/all_to_all | solution.py:107
  81.5 0.8 copy-start
  91.1 16.4 %all-to-all-start.4 = ((bf16[32,2,2048]{2,1,0:T(2,128)(2,1)}), bf16[32,2,2048]{2,1,0:T(2,128)(2,1)}, u32[]{:S(2)}, u32[]{:S(2)}) async-start(bf16[32,2,2048]{2,1,0:T(2,128)(2,1)} %reshape.433), calls=%async_computation.4 | async-start | bytes 524288 | tf_op jit(solution)/shard_map/all_to_all | solution.py:104
  99.5 233.0 %reduce-scatter.2.cloned.1.call-start = ((), (), s32[]{:S(2)}) async-start(), calls=%async_computation.8 | async-start | bytes 2359296 | tf_op jit(solution)/shard_map/reduce_scatter | solution.py:114
  100.5 11.3 %copy-start.2 = (f32[1,32,128,32]{2,1,0,3:T(8,128)}, f32[1,32,128,32]{2,1,0,3:T(8,128)S(1)}, u32[]{:S(2)}) copy-start(f32[1,32,128,32]{2,1,0,3:T(8,128)S(1)} %copy.207) | copy-start | bytes 1572868
  128.5 1.3 copy-start.7
  129.7 1.3 copy-start.6
  132.2 1.3 copy-start.4
  132.2 1.5 copy-start.5
  191.9 2.6 copy-start.1
  222.3 50.1 %all-to-all-start.6 = ((bf16[32,2,2048]{2,1,0:T(2,128)(2,1)}), bf16[32,2,2048]{2,1,0:T(2,128)(2,1)}, u32[]{:S(2)}, u32[]{:S(2)}) async-start(bf16[32,2,2048]{2,1,0:T(2,128)(2,1)} %reshape.437), calls=%async_computation.6 | async-start | bytes 524288 | tf_op jit(solution)/shard_map/all_to_all | solution.py:121
  255.5 4.2 %copy-start.8 = (f32[1,64,128,32]{2,1,3,0:T(8,128)S(1)}, f32[1,64,128,32]{2,1,3,0:T(8,128)}, u32[]{:S(2)}) copy-start(f32[1,64,128,32]{2,1,3,0:T(8,128)} %get-tuple-element.47) | copy-start | bytes 3145732
  269.8 11.3 %copy-start.3 = (f32[1,32,128,32]{2,1,0,3:T(8,128)S(1)}, f32[1,32,128,32]{2,1,0,3:T(8,128)}, u32[]{:S(2)}) copy-start(f32[1,32,128,32]{2,1,0,3:T(8,128)} %copy-done.2) | copy-start | bytes 1572868
  272.4 35.9 %all-to-all-start.5 = ((bf16[32,2,2048]{2,1,0:T(2,128)(2,1)}), bf16[32,2,2048]{2,1,0:T(2,128)(2,1)S(1)}, u32[]{:S(2)}, u32[]{:S(2)}) async-start(bf16[32,2,2048]{2,1,0:T(2,128)(2,1)} %reshape.435), calls=%async_computation.5 | async-start | bytes 524288 | tf_op jit(solution)/shard_map/all_to_all | solution.py:120
  308.3 19.7 %all-to-all-start.3 = ((bf16[32,2,2048]{2,1,0:T(2,128)(2,1)}), bf16[32,2,2048]{2,1,0:T(2,128)(2,1)S(1)}, u32[]{:S(2)}, u32[]{:S(2)}) async-start(bf16[32,2,2048]{2,1,0:T(2,128)(2,1)} %reshape.431), calls=%async_computation.3 | async-start | bytes 524288 | tf_op jit(solution)/shard_map/all_to_all | solution.py:119
Sparse Core Ops, SparseCore 0:
  175.3 42.6 reduce-scatter.1
where the time goes:
time: 346 us; the launch traced here: 341 us
  local copies, waits for them, and re-layouts  111 us (32%)
  other arithmetic  86.2 us (25%)
  matrix products  67.4 us (19%)
  starting transfers between devices  58.8 us (17%)
  between operations  15.2 us (4%)
    unnamed x7, other arithmetic  79.8 us
    unnamed x51, local copies, waits for them, and re-layouts  42 us
    dot_general x24, matrix products, middle_mix(): return jnp.einsum('bjc,jk->bkc', block, table, precision=HIGHEST)  39.5 us
    dot_general x3, matrix products, inverse_real(): jnp.dot(inner_im, folded_im, precision=HIGHEST)  11.9 us
    dot_general x3, matrix products, inverse_real(): jnp.dot(inner_re, folded_re, precision=HIGHEST)  11.1 us
    add x3, local copies, waits for them, and re-layouts, inverse_real(): turned_re = back_re * twist_re + back_im * twist_im  10.3 us
    all_to_all x1, starting transfers between devices, on_device(): lax.all_to_all(key_proj, 'ctx', split_axis=2, concat_axis=1, tiled=True)  9.38 us
    all_to_all x1, starting transfers between devices, on_device(): lax.all_to_all(value_proj, 'ctx', split_axis=2, concat_axis=1, tiled=True)  9.09 us
  transfers between devices with their start and end apart: 8, of which 1 were waited for; matrix products, arithmetic and copies ran while one was open for 56% of the time, Pallas kernels for 0%

commit v1 on v0

v1 whole, which is shorter than its diff:
```python
import functools
import math

import jax
import jax.numpy as jnp
import ml_dtypes
import numpy as np
from jax import lax
from jax.experimental import pallas as pl
from jax.experimental.pallas import tpu as pltpu
from jax.sharding import PartitionSpec as P

MESH = pl.DeviceIdType.MESH
F32 = jnp.float32
BF16 = jnp.bfloat16

N1 = 32
N2 = 128
LENGTH = N1 * N2
GROUP = 4


def high_low(table):
    high = table.astype(ml_dtypes.bfloat16)
    low = (table - high.astype(np.float64)).astype(ml_dtypes.bfloat16)
    return high, low


@functools.lru_cache(maxsize=None)
def tables():
    row = np.arange(N1)
    col = np.arange(N2)
    outer = 2 * np.pi * np.outer(row + 0.25, row) / N1
    first = np.concatenate([np.cos(outer), -np.sin(outer)], axis=0)
    first_high, first_low = high_low(first)
    first_both = np.concatenate([first_high, first_low], axis=1)
    last = np.concatenate([np.cos(outer.T), -np.sin(outer.T)], axis=1) / LENGTH
    last_high, last_low = high_low(last)
    last_all = np.concatenate([last_high, last_high, last_low], axis=1)
    turn = 2 * np.pi * np.outer(row + 0.25, col) / LENGTH
    twist = np.stack([np.cos(turn), -np.sin(turn)]).astype(np.float32)
    inner = 2 * np.pi * (np.outer(col, col) % N2) / N2
    cos, sin = np.cos(inner), np.sin(inner)
    forward = np.block([[cos, -sin], [sin, cos]])
    inverse = np.block([[cos, sin], [-sin, cos]])
    stacked = np.stack(high_low(forward) + high_low(inverse))
    return first_both, last_all, twist, stacked


def place():
    dp = lax.axis_index("dp")
    ctx = lax.axis_index("ctx")
    return dp // 2, dp % 2, ctx


def peer_of(step, core, ctx):
    off = step // 2
    x, z, y = ctx // 8, (ctx // 4) % 2, ctx % 4
    there = ((x + off // 8) % 4) * 8 + ((z + (off // 4) % 2) % 2) * 4 + (y + off % 4) % 4
    return (core + step % 2) % 2, there


def send_kernel(query, key, value, grad, landed, packed, local_sem, send_sem, recv_sem):
    z_hi, core, ctx = place()
    barrier = pltpu.get_barrier_semaphore()

    def greet(step, carry):
        core_to, ctx_to = peer_of(step, core, ctx)
        pl.semaphore_signal(barrier, inc=1, device_id=(z_hi * 2 + core_to, ctx_to), device_id_type=MESH)
        return carry

    lax.fori_loop(1, 64, greet, 0)

    for block in range(8):
        lanes = slice(128 * block, 128 * block + 128)
        for array, (first, second) in enumerate(((key, value), (grad, query))):
            gated = first[:, lanes].astype(F32) * second[:, lanes].astype(F32)
            turned = gated.T.astype(BF16)
            for part in range(8):
                packed[4 * block + part // 2, part % 2, array] = turned[16 * part : 16 * part + 16]

    pl.semaphore_wait(barrier, 63)
    own = pltpu.make_async_copy(packed.at[ctx, core], landed.at[ctx, core], local_sem)
    own.start()

    def copy_to(step):
        core_to, ctx_to = peer_of(step, core, ctx)
        return pltpu.make_async_remote_copy(
            src_ref=packed.at[ctx_to, core_to],
            dst_ref=landed.at[ctx, core],
            send_sem=send_sem.at[step],
            recv_sem=recv_sem.at[ctx * 2 + core],
            device_id=(z_hi * 2 + core_to, ctx_to),
            device_id_type=MESH,
        )

    def send(step, carry):
        copy_to(step).start()
        return carry

    lax.fori_loop(1, 64, send, 0)

    def receive(step, carry):
        core_to, ctx_to = peer_of(step, core, ctx)
        pltpu.make_async_remote_copy(
            src_ref=packed.at[ctx_to, core_to],
            dst_ref=landed.at[ctx_to, core_to],
            send_sem=send_sem.at[step],
            recv_sem=recv_sem.at[ctx_to * 2 + core_to],
            device_id=(z_hi * 2 + core_to, ctx_to),
            device_id_type=MESH,
        ).wait()
        return carry

    lax.fori_loop(1, 64, receive, 0)
    own.wait()


def split(value):
    high = value.astype(BF16)
    return high, (value - high.astype(F32)).astype(BF16)


def dot(left, right):
    return lax.dot_general(left, right, (((1,), (0,)), ((), ())), preferred_element_type=F32)


def middle(value, high, low):
    value_high, value_low = split(value)
    return dot(value_high, high) + dot(value_low, high) + dot(value_high, low)


def twisted(value, twist):
    re, im = value[:N1], value[N1:]
    return jnp.concatenate([re * twist[0] - im * twist[1], re * twist[1] + im * twist[0]], axis=1)


def untwisted(value, twist):
    re, im = value[:, :N2], value[:, N2:]
    return jnp.concatenate([re * twist[0] + im * twist[1], im * twist[0] - re * twist[1]], axis=0)


def convolve_kernel(
    scale, landed, taps, first_both, last_all, twist_ref, mats, back, kernel_part, signals, filters, spectra, results, sums
):
    core = lax.axis_index("dp") % 2
    twist = (twist_ref[0], twist_ref[1])

    def unpack(n1, carry):
        signals[pl.ds(pl.multiple_of(n1 * 64, 64), 64)] = landed[n1].reshape(64, N2).astype(F32)
        rows = taps[pl.ds(pl.multiple_of(n1 * N2, N2), N2)].T
        filters[pl.ds(pl.multiple_of(n1 * 16, 16), 16)] = jnp.where(core == 0, rows[:16], rows[16:])
        return carry

    lax.fori_loop(0, N1, unpack, 0)

    def work(group, carry):
        forward = []
        for pair in range(GROUP // 2):
            channels = [group * GROUP + 2 * pair, group * GROUP + 2 * pair + 1]
            rows = [filters[pl.ds(c, N1, stride=16)] for c in channels]
            high, low = split(jnp.concatenate(rows, axis=1))
            left = first_both[...]
            out = dot(left, jnp.concatenate([high, high], axis=0)) + dot(left[:, :N1], low)
            forward += [twisted(out[:, :N2], twist), twisted(out[:, N2:], twist)]
        for item in range(GROUP):
            c = group * GROUP + item
            for pair in range(2):
                rows = [signals[pl.ds(c + 16 * (2 * s + pair), N1, stride=64)] for s in range(2)]
                data = jnp.concatenate(rows, axis=1).astype(BF16)
                out = dot(first_both[...], jnp.concatenate([data, data], axis=0))
                forward += [twisted(out[:, :N2], twist), twisted(out[:, N2:], twist)]
        spectra[...] = middle(jnp.concatenate(forward, axis=0), mats[0], mats[1])

        def spectrum(index):
            block = spectra[N1 * index : N1 * index + N1]
            return block[:, :N2], block[:, N2:]

        inverse = []
        for item in range(GROUP):
            h_re, h_im = spectrum(item)
            w_re, w_im = 0.0, 0.0
            for s in range(2):
                u_re, u_im = spectrum(GROUP + 4 * item + s)
                m_re, m_im = spectrum(GROUP + 4 * item + 2 + s)
                inverse.append(jnp.concatenate([h_re * u_re - h_im * u_im, h_re * u_im + h_im * u_re], axis=1))
                inverse.append(jnp.concatenate([m_re * h_re + m_im * h_im, m_im * h_re - m_re * h_im], axis=1))
                w_re = w_re + m_re * u_re + m_im * u_im
                w_im = w_im + m_im * u_re - m_re * u_im
            inverse.append(jnp.concatenate([w_re, w_im], axis=1))
        results[...] = middle(jnp.concatenate(inverse, axis=0), mats[2], mats[3])

        def finish(indices):
            turned = [untwisted(results[N1 * i : N1 * i + N1], twist) for i in indices]
            high, low = split(jnp.concatenate(turned, axis=1))
            out = dot(last_all[...], jnp.concatenate([high, low, high], axis=0))
            return out[:, :N2], out[:, N2:]

        for item in range(GROUP):
            c = group * GROUP + item
            for s in range(2):
                conv, inner = finish((5 * item + 2 * s, 5 * item + 2 * s + 1))
                signals[pl.ds(c + 32 * s, N1, stride=64)] = conv
                signals[pl.ds(c + 32 * s + 16, N1, stride=64)] = inner
        for pair in range(GROUP // 2):
            c = group * GROUP + 2 * pair
            parts = finish((10 * pair + 4, 10 * pair + 9))
            sums[pl.ds(c, N1, stride=16)] = parts[0] * scale
            sums[pl.ds(c + 1, N1, stride=16)] = parts[1] * scale
        return carry

    lax.fori_loop(0, 16 // GROUP, work, 0)

    def pack(n1, carry):
        rows = signals[pl.ds(pl.multiple_of(n1 * 64, 64), 64)].astype(BF16)
        back[n1] = rows.reshape(2, 2, 16, N2)
        kernel_part[n1] = sums[pl.ds(pl.multiple_of(n1 * 16, 16), 16)].astype(BF16)
        return carry

    lax.fori_loop(0, N1, pack, 0)


def return_kernel(back, kernel_part, landed, gathered, local_sem, send_sem, recv_sem, part_send, part_recv):
    z_hi, core, ctx = place()
    barrier = pltpu.get_barrier_semaphore()

    def greet(step, carry):
        core_to, ctx_to = peer_of(step, core, ctx)
        pl.semaphore_signal(barrier, inc=1, device_id=(z_hi * 2 + core_to, ctx_to), device_id_type=MESH)
        return carry

    lax.fori_loop(1, 64, greet, 0)

    def greet_far(step, carry):
        z_to, core_to = (z_hi + step // 2) % 4, (core + step % 2) % 2
        pl.semaphore_signal(barrier, inc=1, device_id=(z_to * 2 + core_to, ctx), device_id_type=MESH)
        return carry

    lax.fori_loop(2, 8, greet_far, 0)
    pl.semaphore_wait(barrier, 69)

    def part_copy(step, here):
        z_to, core_to = (z_hi + step // 2) % 4, (core + step % 2) % 2
        to = z_to * 2 + core_to
        slot_z, slot_core = (z_hi, core) if here else (z_to, core_to)
        return pltpu.make_async_remote_copy(
            src_ref=kernel_part.at[pl.ds(to * 4, 4)],
            dst_ref=gathered.at[slot_core, slot_z],
            send_sem=part_send.at[step],
            recv_sem=part_recv.at[slot_z * 2 + slot_core],
            device_id=(to, ctx),
            device_id_type=MESH,
        )

    def copy(step, here):
        core_to, ctx_to = peer_of(step, core, ctx)
        slot_core, slot_ctx = (core, ctx) if here else (core_to, ctx_to)
        return pltpu.make_async_remote_copy(
            src_ref=back.at[ctx_to, core_to],
            dst_ref=landed.at[:, slot_ctx, slot_core],
            send_sem=send_sem.at[step],
            recv_sem=recv_sem.at[slot_ctx * 2 + slot_core],
            device_id=(z_hi * 2 + core_to, ctx_to),
            device_id_type=MESH,
        )

    def start_part(step, carry):
        part_copy(step, True).start()
        return carry

    def start(step, carry):
        copy(step, True).start()
        return carry

    lax.fori_loop(1, 8, start_part, 0)
    lax.fori_loop(1, 64, start, 0)
    own = pltpu.make_async_copy(back.at[ctx, core], landed.at[:, ctx, core], local_sem.at[0])
    own_part = pltpu.make_async_copy(
        kernel_part.at[pl.ds((z_hi * 2 + core) * 4, 4)], gathered.at[core, z_hi], local_sem.at[1]
    )
    own.start()
    own_part.start()

    def finish(step, carry):
        copy(step, False).wait()
        return carry

    def finish_part(step, carry):
        part_copy(step, False).wait()
        return carry

    lax.fori_loop(1, 64, finish, 0)
    lax.fori_loop(1, 8, finish_part, 0)
    own.wait()
    own_part.wait()


def gate_kernel(landed, gathered, query, key, value, grad, query_grad, key_grad, value_grad, taps_grad):
    for block in range(8):
        lanes = slice(128 * block, 128 * block + 128)
        conv = landed[0, 4 * block : 4 * block + 4].reshape(128, N2).astype(F32).T
        inner = landed[1, 4 * block : 4 * block + 4].reshape(128, N2).astype(F32).T
        query_grad[:, lanes] = (conv * grad[:, lanes].astype(F32)).astype(BF16)
        key_grad[:, lanes] = (inner * value[:, lanes].astype(F32)).astype(BF16)
        value_grad[:, lanes] = (inner * key[:, lanes].astype(F32)).astype(BF16)
    for n1 in range(4):
        total = gathered[0, 0, n1].astype(F32), gathered[1, 0, n1].astype(F32)
        for z in range(1, 4):
            total = (total[0] + gathered[0, z, n1].astype(F32), total[1] + gathered[1, z, n1].astype(F32))
        taps_grad[128 * n1 : 128 * n1 + 128] = jnp.concatenate(total, axis=0).T


def on_device(query_proj, key_proj, value_proj, out_grad, filter_taps):
    rows = query_proj.shape[1]
    query, key, value, grad = (a.reshape(rows, -1) for a in (query_proj, key_proj, value_proj, out_grad))
    vmem = pl.BlockSpec(memory_space=pltpu.VMEM)
    limit = 48 * 1024 * 1024
    slabs = jax.ShapeDtypeStruct((N1, 2, 2, 16, N2), BF16)
    landed = pl.pallas_call(
        send_kernel,
        out_shape=slabs,
        in_specs=[vmem] * 4,
        out_specs=vmem,
        scratch_shapes=[
            pltpu.VMEM((N1, 2, 2, 16, N2), BF16),
            pltpu.SemaphoreType.DMA,
            pltpu.SemaphoreType.DMA((64,)),
            pltpu.SemaphoreType.DMA((64,)),
        ],
        compiler_params=pltpu.CompilerParams(collective_id=0, has_side_effects=True, vmem_limit_bytes=limit),
        name="send_gated",
    )(query, key, value, grad)
    scale = 1.0 / math.sqrt(lax.axis_size("dp") * LENGTH)
    back, kernel_part = pl.pallas_call(
        functools.partial(convolve_kernel, scale),
        out_shape=(slabs, jax.ShapeDtypeStruct((N1, 16, N2), BF16)),
        in_specs=[vmem] * 6,
        out_specs=(vmem, vmem),
        scratch_shapes=[
            pltpu.VMEM((N1 * 64, N2), F32),
            pltpu.VMEM((N1 * 16, N2), F32),
            pltpu.VMEM((5 * GROUP * N1, 2 * N2), F32),
            pltpu.VMEM((5 * GROUP * N1, 2 * N2), F32),
            pltpu.VMEM((N1 * 16, N2), F32),
        ],
        compiler_params=pltpu.CompilerParams(vmem_limit_bytes=limit),
        name="convolve",
    )(landed, filter_taps, *(jnp.asarray(t) for t in tables()))
    returned, gathered = pl.pallas_call(
        return_kernel,
        out_shape=(
            jax.ShapeDtypeStruct((2, N1, 2, 16, N2), BF16),
            jax.ShapeDtypeStruct((2, 4, 4, 16, N2), BF16),
        ),
        in_specs=[vmem] * 2,
        out_specs=(vmem, vmem),
        scratch_shapes=[
            pltpu.SemaphoreType.DMA((2,)),
            pltpu.SemaphoreType.DMA((64,)),
            pltpu.SemaphoreType.DMA((64,)),
            pltpu.SemaphoreType.DMA((8,)),
            pltpu.SemaphoreType.DMA((8,)),
        ],
        compiler_params=pltpu.CompilerParams(collective_id=1, has_side_effects=True, vmem_limit_bytes=limit),
        name="send_back",
    )(back, kernel_part)
    flat = jax.ShapeDtypeStruct(query.shape, BF16)
    outs = pl.pallas_call(
        gate_kernel,
        out_shape=(flat, flat, flat, jax.ShapeDtypeStruct((4 * N2, 32), F32)),
        in_specs=[vmem] * 6,
        out_specs=(vmem,) * 4,
        compiler_params=pltpu.CompilerParams(vmem_limit_bytes=limit),
        name="gate",
    )(returned, gathered, query, key, value, grad)
    return tuple(o.reshape(query_proj.shape) for o in outs[:3]) + (outs[3],)


def solution(mesh):
    placed = (P("dp", "ctx", None),) * 4 + (P(None, "ctx"),)
    return jax.shard_map(
        on_device,
        mesh=mesh,
        in_specs=placed,
        out_specs=(P("dp", "ctx", None),) * 3 + (P("dp", "ctx"),),
        check_vma=False,
    )
```

time: 346 us -> 63.5 us (0.18)
  the two profiles are of different devices: /device:TPU:2 before, /device:TPU:1 now
where the time goes in v1:
time: 63.5 us; the launch traced here: 63.3 us
  Pallas kernels  56.3 us (89%)
  local copies, waits for them, and re-layouts  6.21 us (10%)
  between operations  0.77 us (1%)
    pallas_call x1, Pallas kernels, on_device(): pl.pallas_call(return_kernel, out_shape=(jax.ShapeDtypeStruct((2, N1, 2,...  24.4 us
    pallas_call x1, Pallas kernels, on_device(): pl.pallas_call(send_kernel, out_shape=slabs, in_specs=[vmem] * 4, out_spe...  21.7 us
    pallas_call x1, Pallas kernels, on_device(): pl.pallas_call(functools.partial(convolve_kernel, scale), out_shape=(slab...  8.98 us
    unnamed x26, local copies, waits for them, and re-layouts  6.21 us

profile of v1, /device:TPU:1, one launch (start us, length us, event | category | flops | bytes accessed | tf_op | source)
XLA Modules:
  0.0 63.3 jit_solution(15159954632212878443)
XLA Ops:
  0.6 0.0 copy-start
  0.6 0.9 %copy-done = bf16[1,128,1024]{2,1,0:T(8,128)(2,1)S(1)} copy-done((bf16[1,128,1024]{2,1,0:T(8,128)(2,1)S(1)}, bf16[1,128,1024]{2,1,0:T(8,128)(2,1)}, u32[]{:S(2)}) %copy-start) | copy-done | bytes 262168
  1.6 0.0 copy-start.2
  1.6 0.9 %copy-done.2 = bf16[1,128,1024]{2,1,0:T(8,128)(2,1)S(1)} copy-done((bf16[1,128,1024]{2,1,0:T(8,128)(2,1)S(1)}, bf16[1,128,1024]{2,1,0:T(8,128)(2,1)}, u32[]{:S(2)}) %copy-start.2) | copy-done | bytes 262168
  2.5 0.0 copy-start.4
  2.5 0.9 %copy-done.4 = bf16[1,128,1024]{2,1,0:T(8,128)(2,1)S(1)} copy-done((bf16[1,128,1024]{2,1,0:T(8,128)(2,1)S(1)}, bf16[1,128,1024]{2,1,0:T(8,128)(2,1)}, u32[]{:S(2)}) %copy-start.4) | copy-done | bytes 262168
  3.5 0.0 copy-start.6
  3.5 0.9 %copy-done.6 = bf16[1,128,1024]{2,1,0:T(8,128)(2,1)S(1)} copy-done((bf16[1,128,1024]{2,1,0:T(8,128)(2,1)S(1)}, bf16[1,128,1024]{2,1,0:T(8,128)(2,1)}, u32[]{:S(2)}) %copy-start.6) | copy-done | bytes 262168
  4.4 0.0 copy-start.8
  4.4 0.0 copy-start.9
  4.4 0.0 copy-start.10
  4.4 0.0 copy-start.11
  4.4 21.7 %send_gated.1.landed = bf16[32,2,2,16,128]{4,3,2,1,0:T(8,128)(2,1)S(1)} custom-call(bf16[128,1024]{1,0:T(8,128)(2,1)S(1)} %bitcast.7, bf16[128,1024]{1,0:T(8,128)(2,1)S(1)} %bitcast.9, bf16[128,1024]{1,0:T(8,128)(2,1)S(1)} %bitcast.11, bf16[128,1024]{1,0:T(8,128)(2,1)S(1)} %bitcast.13), custom_call_target="tpu_custom_call" | custom-call | tf_op jit(solution)/shard_map/send_gated/pallas_call | solution.py:319
  26.2 1.6 %copy.13.taps = f32[4096,32]{1,0:T(8,128)S(1)} copy(f32[4096,32]{0,1:T(8,128)} %param.13) | data formatting | bytes 1048576 | tf_op args[4]
  27.8 0.0 copy-done.8
  27.8 0.0 copy-done.9
  27.9 0.0 copy-done.10
  27.9 0.0 copy-done.11
  27.9 0.0 copy-start.1
  27.9 0.0 copy-start.3
  27.9 0.0 copy-start.5
  27.9 0.0 copy-start.7
  27.9 9.0 %convolve.1 = (bf16[32,2,2,16,128]{4,3,2,1,0:T(8,128)(2,1)S(1)}, bf16[32,16,128]{2,1,0:T(8,128)(2,1)S(1)}) custom-call(bf16[32,2,2,16,128]{4,3,2,1,0:T(8,128)(2,1)S(1)} %send_gated.1.landed, f32[4096,32]{1,0:T(8,128)S(1)} %copy.13.taps, bf16[64,64]{1,0:T(8,128)(2,1)S(1)} %copy-done.11, bf16[32,192]{1,0:T(8,128)(2,1)S(1)} %copy-done.10, ...), custom_call_target="tpu_custom_call" | custom-call | tf_op jit(solution)/shard_map/convolve/pallas_call | solution.py:334
  36.9 24.4 %send_back.1 = (bf16[2,32,2,16,128]{4,3,2,1,0:T(8,128)(2,1)S(1)}, bf16[2,4,4,16,128]{4,3,2,1,0:T(8,128)(2,1)S(1)}) custom-call(bf16[32,2,2,16,128]{4,3,2,1,0:T(8,128)(2,1)S(1)} %get-tuple-element.12.back, bf16[32,16,128]{2,1,0:T(8,128)(2,1)S(1)} %get-tuple-element.13.kernel_part), custom_call_target="tpu_custom_call" | custom-call | tf_op jit(solution)/shard_map/send_back/pallas_call | solution.py:349
  61.4 0.0 copy-done.1
  61.4 0.0 copy-done.3
  61.4 0.0 copy-done.5
  61.4 0.0 copy-done.7
  61.4 1.2 %gate.1 = (bf16[128,1024]{1,0:T(8,128)(2,1)}, bf16[128,1024]{1,0:T(8,128)(2,1)}, bf16[128,1024]{1,0:T(8,128)(2,1)}, f32[512,32]{1,0:T(8,128)S(1)}) custom-call(bf16[2,32,2,16,128]{4,3,2,1,0:T(8,128)(2,1)S(1)} %get-tuple-element.14.landed, bf16[2,4,4,16,128]{4,3,2,1,0:T(8,128)(2,1)S(1)} %get-tuple-element.15.gathered, bf16[128,1024]{1,0:T(8,128)(2,1)S(1)} %bitcast.8, ...), custom_call_target="tpu_custom_call" | custom-call | tf_op jit(solution)/shard_map/gate/pallas_call | solution.py:368
  62.5 0.7 %copy.14 = f32[512,32]{0,1:T(8,128)} copy(f32[512,32]{1,0:T(8,128)S(1)} %get-tuple-element.23) | data formatting | bytes 131072
Async XLA Ops:
  0.6 1.0 %copy-start = (bf16[1,128,1024]{2,1,0:T(8,128)(2,1)S(1)}, bf16[1,128,1024]{2,1,0:T(8,128)(2,1)}, u32[]{:S(2)}) copy-start(bf16[1,128,1024]{2,1,0:T(8,128)(2,1)} %param.9) | copy-start | bytes 786436
  1.6 0.9 %copy-start.2 = (bf16[1,128,1024]{2,1,0:T(8,128)(2,1)S(1)}, bf16[1,128,1024]{2,1,0:T(8,128)(2,1)}, u32[]{:S(2)}) copy-start(bf16[1,128,1024]{2,1,0:T(8,128)(2,1)} %param.10) | copy-start | bytes 786436
  2.5 0.9 %copy-start.4 = (bf16[1,128,1024]{2,1,0:T(8,128)(2,1)S(1)}, bf16[1,128,1024]{2,1,0:T(8,128)(2,1)}, u32[]{:S(2)}) copy-start(bf16[1,128,1024]{2,1,0:T(8,128)(2,1)} %param.11) | copy-start | bytes 786436
  3.5 0.9 %copy-start.6 = (bf16[1,128,1024]{2,1,0:T(8,128)(2,1)S(1)}, bf16[1,128,1024]{2,1,0:T(8,128)(2,1)}, u32[]{:S(2)}) copy-start(bf16[1,128,1024]{2,1,0:T(8,128)(2,1)} %param.12) | copy-start | bytes 786436
  4.4 23.4 %copy-start.8 = (bf16[4,256,256]{2,1,0:T(8,128)(2,1)S(1)}, bf16[4,256,256]{2,1,0:T(8,128)(2,1)}, u32[]{:S(2)}) copy-start(bf16[4,256,256]{2,1,0:T(8,128)(2,1)} %constant.11.clone.mats) | copy-start | bytes 1572868
  4.4 23.4 %copy-start.9 = (f32[2,32,128]{2,1,0:T(8,128)S(1)}, f32[2,32,128]{2,1,0:T(8,128)}, u32[]{:S(2)}) copy-start(f32[2,32,128]{2,1,0:T(8,128)} %constant.10.clone.twist_ref) | copy-start | bytes 98308
  4.4 23.4 %copy-start.10 = (bf16[32,192]{1,0:T(8,128)(2,1)S(1)}, bf16[32,192]{1,0:T(8,128)(2,1)}, u32[]{:S(2)}) copy-start(bf16[32,192]{1,0:T(8,128)(2,1)} %constant.9.clone.last_all) | copy-start | bytes 36868
  4.4 23.4 %copy-start.11 = (bf16[64,64]{1,0:T(8,128)(2,1)S(1)}, bf16[64,64]{1,0:T(8,128)(2,1)}, u32[]{:S(2)}) copy-start(bf16[64,64]{1,0:T(8,128)(2,1)} %constant.8.clone.first_both) | copy-start | bytes 24580
  27.9 33.5 %copy-start.1 = (bf16[1,128,1024]{2,1,0:T(8,128)(2,1)S(1)}, bf16[1,128,1024]{2,1,0:T(8,128)(2,1)}, u32[]{:S(2)}) copy-start(bf16[1,128,1024]{2,1,0:T(8,128)(2,1)} %param.9) | copy-start | bytes 786436
  27.9 33.5 %copy-start.3 = (bf16[1,128,1024]{2,1,0:T(8,128)(2,1)S(1)}, bf16[1,128,1024]{2,1,0:T(8,128)(2,1)}, u32[]{:S(2)}) copy-start(bf16[1,128,1024]{2,1,0:T(8,128)(2,1)} %param.10) | copy-start | bytes 786436
  27.9 33.5 %copy-start.5 = (bf16[1,128,1024]{2,1,0:T(8,128)(2,1)S(1)}, bf16[1,128,1024]{2,1,0:T(8,128)(2,1)}, u32[]{:S(2)}) copy-start(bf16[1,128,1024]{2,1,0:T(8,128)(2,1)} %param.11) | copy-start | bytes 786436
  27.9 33.5 %copy-start.7 = (bf16[1,128,1024]{2,1,0:T(8,128)(2,1)S(1)}, bf16[1,128,1024]{2,1,0:T(8,128)(2,1)}, u32[]{:S(2)}) copy-start(bf16[1,128,1024]{2,1,0:T(8,128)(2,1)} %param.12) | copy-start | bytes 786436

commit v2 on v0

v2 whole, which is shorter than its diff:
```python
import functools
import math

import jax
import jax.numpy as jnp
import ml_dtypes
import numpy as np
from jax import lax
from jax.experimental import pallas as pl
from jax.experimental.pallas import tpu as pltpu
from jax.sharding import PartitionSpec as P

MESH = pl.DeviceIdType.MESH
F32 = jnp.float32
BF16 = jnp.bfloat16

N1 = 32
N2 = 128
LENGTH = N1 * N2
GROUP = 8
HALF = 16


def high_low(table):
    high = table.astype(ml_dtypes.bfloat16)
    low = (table - high.astype(np.float64)).astype(ml_dtypes.bfloat16)
    return high, low


@functools.lru_cache(maxsize=None)
def tables():
    row = np.arange(N1)
    col = np.arange(N2)
    outer = 2 * np.pi * np.outer(row + 0.25, row) / N1
    first = np.concatenate([np.cos(outer), -np.sin(outer)], axis=0)
    first_high, first_low = high_low(first)
    first_both = np.concatenate([first_high, first_low], axis=1)
    last = np.concatenate([np.cos(outer.T), -np.sin(outer.T)], axis=1) / LENGTH
    last_high, last_low = high_low(last)
    last_all = np.concatenate([last_high, last_high, last_low], axis=1)
    turn = 2 * np.pi * np.outer(row + 0.25, col) / LENGTH
    twist = np.stack([np.cos(turn), -np.sin(turn)]).astype(np.float32)
    inner = 2 * np.pi * (np.outer(col, col) % N2) / N2
    cos, sin = np.cos(inner), np.sin(inner)
    forward = np.block([[cos, -sin], [sin, cos]])
    inverse = np.block([[cos, sin], [-sin, cos]])
    stacked = np.stack(high_low(forward) + high_low(inverse))
    return first_both, last_all, twist, stacked


def place():
    dp = lax.axis_index("dp")
    ctx = lax.axis_index("ctx")
    return dp // 2, dp % 2, ctx


def gray(j):
    return j + (j // 2) * (1 - 2 * (j % 2))


def peer_of(step, ctx):
    x, z, y = ctx // 8, (ctx // 4) % 2, ctx % 4
    return ((x + gray(step // 8)) % 4) * 8 + ((z + step % 2) % 2) * 4 + (y + gray((step // 2) % 4)) % 4


def split(value):
    high = value.astype(BF16)
    return high, (value - high.astype(F32)).astype(BF16)


def dot(left, right):
    return lax.dot_general(left, right, (((1,), (0,)), ((), ())), preferred_element_type=F32)


def middle(value, high, low):
    value_high, value_low = split(value)
    return dot(value_high, high) + dot(value_low, high) + dot(value_high, low)


def twisted(value, twist):
    re, im = value[:N1], value[N1:]
    return jnp.concatenate([re * twist[0] - im * twist[1], re * twist[1] + im * twist[0]], axis=1)


def untwisted(value, twist):
    re, im = value[:, :N2], value[:, N2:]
    return jnp.concatenate([re * twist[0] + im * twist[1], im * twist[0] - re * twist[1]], axis=0)


def fused_kernel(
    scale, query_hbm, key_hbm, value_hbm, grad_hbm, taps, first_both, last_all, twist_ref, mats, landed, gathered,
    inputs, packed, arrived, back, signals, filters, filter_spectra, spectra, results, sums, pair_sums, parts,
    load_sem, out_send, out_recv, back_send, back_recv, own_sem, pair_send, pair_recv, part_send, part_recv,
):
    z_hi, core, ctx = place()
    dp = z_hi * 2 + core
    pair = (z_hi * 2 + (core + 1) % 2, ctx)
    loads = [
        pltpu.make_async_copy(ref, inputs.at[i], load_sem.at[i])
        for i, ref in enumerate((key_hbm, value_hbm, grad_hbm, query_hbm))
    ]
    for load in loads:
        load.start()

    barrier = pltpu.get_barrier_semaphore()

    def greet(step, carry):
        pl.semaphore_signal(barrier, inc=1, device_id=(dp, peer_of(step, ctx)), device_id_type=MESH)
        return carry

    lax.fori_loop(1, 32, greet, 0)
    pl.semaphore_signal(barrier, inc=1, device_id=pair, device_id_type=MESH)
    for away in range(1, 4):
        there = ((z_hi + away) % 4) * 2 + core
        pl.semaphore_signal(barrier, inc=1, device_id=(there, ctx), device_id_type=MESH)

    def out_copy(half, there, slot):
        return pltpu.make_async_remote_copy(
            src_ref=packed.at[there, half],
            dst_ref=arrived.at[slot, half],
            send_sem=out_send.at[half, there],
            recv_sem=out_recv.at[half, slot],
            device_id=(dp, there),
            device_id_type=MESH,
        )

    def back_copy(half, there, slot):
        return pltpu.make_async_remote_copy(
            src_ref=back.at[there, half],
            dst_ref=landed.at[slot, half],
            send_sem=back_send.at[half, there],
            recv_sem=back_recv.at[half, slot],
            device_id=(dp, there),
            device_id_type=MESH,
        )

    def pair_copy(half, z):
        return pltpu.make_async_remote_copy(
            src_ref=sums.at[half, pl.ds((z * 2 + (core + 1) % 2) * 64, 64)],
            dst_ref=pair_sums.at[half, z],
            send_sem=pair_send.at[half, z],
            recv_sem=pair_recv.at[half, z],
            device_id=pair,
            device_id_type=MESH,
        )

    def part_copy(half, there, slot):
        return pltpu.make_async_remote_copy(
            src_ref=parts.at[half, there],
            dst_ref=gathered.at[half, slot],
            send_sem=part_send.at[half, there],
            recv_sem=part_recv.at[half, slot],
            device_id=(there * 2 + core, ctx),
            device_id_type=MESH,
        )

    def steps(body):
        def run(step, carry):
            body(peer_of(31 - step, ctx))
            return carry

        lax.fori_loop(0, 31, run, 0)

    for load in loads:
        load.wait()
    x, z_lo = ctx // 8, (ctx // 4) % 2
    for order, (dx, dz) in enumerate(((2, 1), (2, 0), (1, 1), (3, 1), (1, 0), (3, 0), (0, 1), (0, 0))):
        block = ((x + dx) % 4) * 2 + (z_lo + dz) % 2
        lanes = pl.ds(pl.multiple_of(128 * block, 128), 128)
        for array in range(2):
            gated = inputs[2 * array, :, lanes].astype(F32) * inputs[2 * array + 1, :, lanes].astype(F32)
            turned = gated.T.astype(BF16)
            for part in range(8):
                packed[4 * block + part // 2, part % 2, array] = turned[16 * part : 16 * part + 16]
        if order == 0:
            pl.semaphore_wait(barrier, 35)
        for dy in (2, 1, 3, 0):
            if dx or dz or dy:
                there = 4 * block + (ctx + dy) % 4
                out_copy(0, there, ctx).start()
    own = [
        pltpu.make_async_copy(packed.at[ctx, half], arrived.at[ctx, half], own_sem.at[half]) for half in range(2)
    ]
    own[0].start()
    own[1].start()
    steps(lambda there: out_copy(1, there, ctx).start())

    twist = (twist_ref[0], twist_ref[1])
    for n1 in range(N1):
        filters[32 * n1 : 32 * n1 + 32] = taps[:, N2 * n1 : N2 * n1 + N2]

    def filter_work(group, carry):
        forward = []
        for item in range(0, GROUP, 2):
            rows = [filters[pl.ds(group * GROUP + item + i, N1, stride=32)] for i in range(2)]
            high, low = split(jnp.concatenate(rows, axis=1))
            left = first_both[...]
            out = dot(left, jnp.concatenate([high, high], axis=0)) + dot(left[:, :N1], low)
            forward += [twisted(out[:, :N2], twist), twisted(out[:, N2:], twist)]
        rows = pl.ds(pl.multiple_of(group * GROUP * N1, GROUP * N1), GROUP * N1)
        filter_spectra[rows] = middle(jnp.concatenate(forward, axis=0), mats[0], mats[1])
        return carry

    lax.fori_loop(0, 2 * HALF // GROUP, filter_work, 0)

    for half in range(2):
        steps(lambda there: out_copy(half, there, there).wait_recv())
        own[half].wait()

        def unpack(n1, carry):
            rows = arrived[n1, half].reshape(32, N2).astype(F32)
            signals[pl.ds(pl.multiple_of(n1 * 32, 32), 32)] = rows
            return carry

        lax.fori_loop(0, N1, unpack, 0)

        def work(group, carry):
            forward = []
            for item in range(GROUP):
                rows = [signals[pl.ds(group * GROUP + item + HALF * i, N1, stride=32)] for i in range(2)]
                data = jnp.concatenate(rows, axis=1).astype(BF16)
                out = dot(first_both[...], jnp.concatenate([data, data], axis=0))
                forward += [twisted(out[:, :N2], twist), twisted(out[:, N2:], twist)]
            spectra[...] = middle(jnp.concatenate(forward, axis=0), mats[0], mats[1])
            inverse = []
            for item in range(GROUP):
                start = (half * HALF + group * GROUP + item) * N1
                h = filter_spectra[pl.ds(pl.multiple_of(start, N1), N1)]
                h_re, h_im = h[:, :N2], h[:, N2:]
                u = spectra[2 * item * N1 : (2 * item + 1) * N1]
                u_re, u_im = u[:, :N2], u[:, N2:]
                m = spectra[(2 * item + 1) * N1 : (2 * item + 2) * N1]
                m_re, m_im = m[:, :N2], m[:, N2:]
                inverse.append(jnp.concatenate([h_re * u_re - h_im * u_im, h_re * u_im + h_im * u_re], axis=1))
                inverse.append(jnp.concatenate([m_re * h_re + m_im * h_im, m_im * h_re - m_re * h_im], axis=1))
                inverse.append(jnp.concatenate([m_re * u_re + m_im * u_im, m_im * u_re - m_re * u_im], axis=1))
            results[...] = middle(jnp.concatenate(inverse, axis=0), mats[2], mats[3])

            def finish(indices):
                turned = [untwisted(results[N1 * i : N1 * i + N1], twist) for i in indices]
                high, low = split(jnp.concatenate(turned, axis=1))
                out = dot(last_all[...], jnp.concatenate([high, low, high], axis=0))
                return out[:, :N2], out[:, N2:]

            for item in range(GROUP):
                c = group * GROUP + item
                conv, inner = finish((3 * item, 3 * item + 1))
                signals[pl.ds(c, N1, stride=32)] = conv
                signals[pl.ds(c + HALF, N1, stride=32)] = inner
            for item in range(0, GROUP, 2):
                c = group * GROUP + item
                first, second = finish((3 * item + 2, 3 * item + 5))
                sums[half, pl.ds(c, N1, stride=HALF)] = first * scale
                sums[half, pl.ds(c + 1, N1, stride=HALF)] = second * scale
            return carry

        lax.fori_loop(0, HALF // GROUP, work, 0)

        def pack(n1, carry):
            rows = signals[pl.ds(pl.multiple_of(n1 * 32, 32), 32)].astype(BF16)
            back[n1, half] = rows.reshape(2, 16, N2)
            return carry

        lax.fori_loop(0, N1, pack, 0)
        for z in range(4):
            pair_copy(half, z).start()
        steps(lambda there: back_copy(half, there, ctx).start())
        landed[ctx, half] = back[ctx, half]
        for z in range(4):
            pair_copy(half, z).wait()
            mine = sums[half, pl.ds(pl.multiple_of((z * 2 + core) * 64, 64), 64)]
            parts[half, z] = (mine + pair_sums[half, z]).astype(BF16)
        for away in (2, 1, 3):
            part_copy(half, (z_hi + away) % 4, z_hi).start()
        gathered[half, z_hi] = parts[half, z_hi]

    for half in range(2):
        steps(lambda there: out_copy(half, there, there).wait_send())
        steps(lambda there: back_copy(half, there, there).wait())
        for away in (2, 1, 3):
            there = (z_hi + away) % 4
            part_copy(half, there, there).wait()


def gate_kernel(landed, gathered, query, key, value, grad, query_grad, key_grad, value_grad, taps_grad):
    for block in range(8):
        lanes = slice(128 * block, 128 * block + 128)
        devices = slice(4 * block, 4 * block + 4)
        conv = landed[devices, :, 0].reshape(128, N2).astype(F32).T
        inner = landed[devices, :, 1].reshape(128, N2).astype(F32).T
        query_grad[:, lanes] = (conv * grad[:, lanes].astype(F32)).astype(BF16)
        key_grad[:, lanes] = (inner * value[:, lanes].astype(F32)).astype(BF16)
        value_grad[:, lanes] = (inner * key[:, lanes].astype(F32)).astype(BF16)
    for half in range(2):
        total = gathered[half, 0].astype(F32)
        for z in range(1, 4):
            total = total + gathered[half, z].astype(F32)
        for n1 in range(4):
            taps_grad[16 * half : 16 * half + 16, N2 * n1 : N2 * n1 + N2] = total[16 * n1 : 16 * n1 + 16]


def on_device(query_proj, key_proj, value_proj, out_grad, filter_taps):
    rows = query_proj.shape[1]
    query, key, value, grad = (a.reshape(rows, -1) for a in (query_proj, key_proj, value_proj, out_grad))
    vmem = pl.BlockSpec(memory_space=pltpu.VMEM)
    anywhere = pl.BlockSpec(memory_space=pl.ANY)
    limit = 40 * 1024 * 1024
    slabs = (N1, 2, 2, HALF, N2)
    scale = 1.0 / math.sqrt(lax.axis_size("dp") * LENGTH)
    dma = pltpu.SemaphoreType.DMA
    landed, gathered = pl.pallas_call(
        functools.partial(fused_kernel, scale),
        out_shape=(jax.ShapeDtypeStruct(slabs, BF16), jax.ShapeDtypeStruct((2, 4, 64, N2), BF16)),
        in_specs=[anywhere] * 4 + [vmem] * 5,
        out_specs=(vmem, vmem),
        scratch_shapes=[
            pltpu.VMEM((4, rows, query.shape[1]), BF16),
            pltpu.VMEM(slabs, BF16),
            pltpu.VMEM(slabs, BF16),
            pltpu.VMEM(slabs, BF16),
            pltpu.VMEM((N1 * 2 * HALF, N2), F32),
            pltpu.VMEM((N1 * 2 * HALF, N2), F32),
            pltpu.VMEM((2 * HALF * N1, 2 * N2), F32),
            pltpu.VMEM((2 * GROUP * N1, 2 * N2), F32),
            pltpu.VMEM((3 * GROUP * N1, 2 * N2), F32),
            pltpu.VMEM((2, N1 * HALF, N2), F32),
            pltpu.VMEM((2, 4, 64, N2), F32),
            pltpu.VMEM((2, 4, 64, N2), BF16),
            dma((4,)),
            dma((2, 32)),
            dma((2, 32)),
            dma((2, 32)),
            dma((2, 32)),
            dma((2,)),
            dma((2, 4)),
            dma((2, 4)),
            dma((2, 4)),
            dma((2, 4)),
        ],
        compiler_params=pltpu.CompilerParams(collective_id=0, has_side_effects=True, vmem_limit_bytes=limit),
        name="exchange_convolve",
    )(query, key, value, grad, filter_taps.T, *(jnp.asarray(t) for t in tables()))
    flat = jax.ShapeDtypeStruct(query.shape, BF16)
    outs = pl.pallas_call(
        gate_kernel,
        out_shape=(flat, flat, flat, jax.ShapeDtypeStruct((2 * HALF, 4 * N2), F32)),
        in_specs=[vmem] * 6,
        out_specs=(vmem,) * 4,
        compiler_params=pltpu.CompilerParams(vmem_limit_bytes=48 * 1024 * 1024),
        name="gate",
    )(landed, gathered, query, key, value, grad)
    return tuple(o.reshape(query_proj.shape) for o in outs[:3]) + (outs[3].T,)


def solution(mesh):
    placed = (P("dp", "ctx", None),) * 4 + (P(None, "ctx"),)
    return jax.shard_map(
        on_device,
        mesh=mesh,
        in_specs=placed,
        out_specs=(P("dp", "ctx", None),) * 3 + (P("dp", "ctx"),),
        check_vma=False,
    )
```

time: 346 us -> 49.6 us (0.14)
  the two profiles are of different devices: /device:TPU:2 before, /device:TPU:1 now
where the time goes in v2:
time: 49.6 us; the launch traced here: 49.1 us
  Pallas kernels  40.3 us (81%)
  local copies, waits for them, and re-layouts  8.08 us (16%)
  between operations  0.69 us (1%)
    pallas_call x1, Pallas kernels, on_device(): pl.pallas_call(functools.partial(fused_kernel, scale), out_shape=(jax.Sha...  39.2 us
    unnamed x26, local copies, waits for them, and re-layouts  8.08 us
    pallas_call x1, Pallas kernels, on_device(): pl.pallas_call(gate_kernel, out_shape=(flat, flat, flat, jax.ShapeDtypeSt...  1.15 us

profile of v2, /device:TPU:1, one launch (start us, length us, event | category | flops | bytes accessed | tf_op | source)
XLA Modules:
  0.0 49.1 jit_solution(3577088776763184350)
XLA Ops:
  0.6 0.0 copy-start
  0.6 0.9 %copy-done = bf16[1,128,1024]{2,1,0:T(8,128)(2,1)S(1)} copy-done((bf16[1,128,1024]{2,1,0:T(8,128)(2,1)S(1)}, bf16[1,128,1024]{2,1,0:T(8,128)(2,1)}, u32[]{:S(2)}) %copy-start) | copy-done | bytes 262168
  1.6 0.0 copy-start.2
  1.6 0.9 %copy-done.2 = bf16[1,128,1024]{2,1,0:T(8,128)(2,1)S(1)} copy-done((bf16[1,128,1024]{2,1,0:T(8,128)(2,1)S(1)}, bf16[1,128,1024]{2,1,0:T(8,128)(2,1)}, u32[]{:S(2)}) %copy-start.2) | copy-done | bytes 262168
  2.5 0.0 copy-start.4
  2.5 0.9 %copy-done.4 = bf16[1,128,1024]{2,1,0:T(8,128)(2,1)S(1)} copy-done((bf16[1,128,1024]{2,1,0:T(8,128)(2,1)S(1)}, bf16[1,128,1024]{2,1,0:T(8,128)(2,1)}, u32[]{:S(2)}) %copy-start.4) | copy-done | bytes 262168
  3.5 0.0 copy-start.6
  3.5 0.9 %copy-done.6 = bf16[1,128,1024]{2,1,0:T(8,128)(2,1)S(1)} copy-done((bf16[1,128,1024]{2,1,0:T(8,128)(2,1)S(1)}, bf16[1,128,1024]{2,1,0:T(8,128)(2,1)}, u32[]{:S(2)}) %copy-start.6) | copy-done | bytes 262168
  4.4 0.0 copy-start.8
  4.4 1.0 %copy-done.8 = f32[4096,32]{0,1:T(8,128)S(1)} copy-done((f32[4096,32]{0,1:T(8,128)S(1)}, f32[4096,32]{0,1:T(8,128)}, u32[]{:S(2)}) %copy-start.8) | copy-done | bytes 524312
  5.5 0.0 copy-start.9
  5.5 1.0 %copy-done.9 = bf16[4,256,256]{2,1,0:T(8,128)(2,1)S(1)} copy-done((bf16[4,256,256]{2,1,0:T(8,128)(2,1)S(1)}, bf16[4,256,256]{2,1,0:T(8,128)(2,1)}, u32[]{:S(2)}) %copy-start.9) | copy-done | bytes 524312
  6.5 0.0 copy-start.10
  6.5 0.8 %copy-done.10 = f32[2,32,128]{2,1,0:T(8,128)S(1)} copy-done((f32[2,32,128]{2,1,0:T(8,128)S(1)}, f32[2,32,128]{2,1,0:T(8,128)}, u32[]{:S(2)}) %copy-start.10) | copy-done | bytes 32792
  7.3 0.0 copy-start.11
  7.3 0.7 %copy-done.11 = bf16[32,192]{1,0:T(8,128)(2,1)S(1)} copy-done((bf16[32,192]{1,0:T(8,128)(2,1)S(1)}, bf16[32,192]{1,0:T(8,128)(2,1)}, u32[]{:S(2)}) %copy-start.11) | copy-done | bytes 12312
  8.0 0.0 copy-start.12
  8.0 0.7 %copy-done.12 = bf16[64,64]{1,0:T(8,128)(2,1)S(1)} copy-done((bf16[64,64]{1,0:T(8,128)(2,1)S(1)}, bf16[64,64]{1,0:T(8,128)(2,1)}, u32[]{:S(2)}) %copy-start.12) | copy-done | bytes 8216
  8.7 0.0 copy-start.1
  8.7 0.0 copy-start.3
  8.7 0.0 copy-start.5
  8.7 0.0 copy-start.7
  8.7 39.2 %exchange_convolve.1 = (bf16[32,2,2,16,128]{4,3,2,1,0:T(8,128)(2,1)S(1)}, bf16[2,4,64,128]{3,2,1,0:T(8,128)(2,1)S(1)}) custom-call(bf16[128,1024]{1,0:T(8,128)(2,1)S(1)} %bitcast.9, bf16[128,1024]{1,0:T(8,128)(2,1)S(1)} %bitcast.11, bf16[128,1024]{1,0:T(8,128)(2,1)S(1)} %bitcast.13, bf16[128,1024]{1,0:T(8,128)(2,1)S(1)} %bitcast.15, ...), custom_call_target="tpu_custom_call" | custom-call | tf_op jit(solution)/shard_map/exchange_convolve/pallas_call | solution.py:311
  47.9 0.0 copy-done.1
  47.9 0.0 copy-done.3
  47.9 0.0 copy-done.5
  47.9 0.0 copy-done.7
  47.9 1.2 %gate.1 = (bf16[128,1024]{1,0:T(8,128)(2,1)}, bf16[128,1024]{1,0:T(8,128)(2,1)}, bf16[128,1024]{1,0:T(8,128)(2,1)}, f32[32,512]{1,0:T(8,128)}) custom-call(bf16[32,2,2,16,128]{4,3,2,1,0:T(8,128)(2,1)S(1)} %get-tuple-element.10.landed, bf16[2,4,64,128]{3,2,1,0:T(8,128)(2,1)S(1)} %get-tuple-element.11.gathered, bf16[128,1024]{1,0:T(8,128)(2,1)S(1)} %bitcast.10, ...), custom_call_target="tpu_custom_call" | custom-call | tf_op jit(solution)/shard_map/gate/pallas_call | solution.py:344
Async XLA Ops:
  0.6 1.0 %copy-start = (bf16[1,128,1024]{2,1,0:T(8,128)(2,1)S(1)}, bf16[1,128,1024]{2,1,0:T(8,128)(2,1)}, u32[]{:S(2)}) copy-start(bf16[1,128,1024]{2,1,0:T(8,128)(2,1)} %param.9) | copy-start | bytes 786436
  1.6 0.9 %copy-start.2 = (bf16[1,128,1024]{2,1,0:T(8,128)(2,1)S(1)}, bf16[1,128,1024]{2,1,0:T(8,128)(2,1)}, u32[]{:S(2)}) copy-start(bf16[1,128,1024]{2,1,0:T(8,128)(2,1)} %param.10) | copy-start | bytes 786436
  2.5 0.9 %copy-start.4 = (bf16[1,128,1024]{2,1,0:T(8,128)(2,1)S(1)}, bf16[1,128,1024]{2,1,0:T(8,128)(2,1)}, u32[]{:S(2)}) copy-start(bf16[1,128,1024]{2,1,0:T(8,128)(2,1)} %param.11) | copy-start | bytes 786436
  3.5 0.9 %copy-start.6 = (bf16[1,128,1024]{2,1,0:T(8,128)(2,1)S(1)}, bf16[1,128,1024]{2,1,0:T(8,128)(2,1)}, u32[]{:S(2)}) copy-start(bf16[1,128,1024]{2,1,0:T(8,128)(2,1)} %param.12) | copy-start | bytes 786436
  4.4 1.0 %copy-start.8 = (f32[4096,32]{0,1:T(8,128)S(1)}, f32[4096,32]{0,1:T(8,128)}, u32[]{:S(2)}) copy-start(f32[4096,32]{0,1:T(8,128)} %param.13) | copy-start | bytes 1572868
  5.5 1.0 %copy-start.9 = (bf16[4,256,256]{2,1,0:T(8,128)(2,1)S(1)}, bf16[4,256,256]{2,1,0:T(8,128)(2,1)}, u32[]{:S(2)}) copy-start(bf16[4,256,256]{2,1,0:T(8,128)(2,1)} %constant.11.clone.mats) | copy-start | bytes 1572868
  6.5 0.8 %copy-start.10 = (f32[2,32,128]{2,1,0:T(8,128)S(1)}, f32[2,32,128]{2,1,0:T(8,128)}, u32[]{:S(2)}) copy-start(f32[2,32,128]{2,1,0:T(8,128)} %constant.10.clone.twist_ref) | copy-start | bytes 98308
  7.3 0.7 %copy-start.11 = (bf16[32,192]{1,0:T(8,128)(2,1)S(1)}, bf16[32,192]{1,0:T(8,128)(2,1)}, u32[]{:S(2)}) copy-start(bf16[32,192]{1,0:T(8,128)(2,1)} %constant.9.clone.last_all) | copy-start | bytes 36868
  8.0 0.7 %copy-start.12 = (bf16[64,64]{1,0:T(8,128)(2,1)S(1)}, bf16[64,64]{1,0:T(8,128)(2,1)}, u32[]{:S(2)}) copy-start(bf16[64,64]{1,0:T(8,128)(2,1)} %constant.8.clone.first_both) | copy-start | bytes 24580
  8.7 39.2 %copy-start.1 = (bf16[1,128,1024]{2,1,0:T(8,128)(2,1)S(1)}, bf16[1,128,1024]{2,1,0:T(8,128)(2,1)}, u32[]{:S(2)}) copy-start(bf16[1,128,1024]{2,1,0:T(8,128)(2,1)} %param.9) | copy-start | bytes 786436
  8.7 39.2 %copy-start.3 = (bf16[1,128,1024]{2,1,0:T(8,128)(2,1)S(1)}, bf16[1,128,1024]{2,1,0:T(8,128)(2,1)}, u32[]{:S(2)}) copy-start(bf16[1,128,1024]{2,1,0:T(8,128)(2,1)} %param.10) | copy-start | bytes 786436
  8.7 39.2 %copy-start.5 = (bf16[1,128,1024]{2,1,0:T(8,128)(2,1)S(1)}, bf16[1,128,1024]{2,1,0:T(8,128)(2,1)}, u32[]{:S(2)}) copy-start(bf16[1,128,1024]{2,1,0:T(8,128)(2,1)} %param.11) | copy-start | bytes 786436
  8.7 39.2 %copy-start.7 = (bf16[1,128,1024]{2,1,0:T(8,128)(2,1)S(1)}, bf16[1,128,1024]{2,1,0:T(8,128)(2,1)}, u32[]{:S(2)}) copy-start(bf16[1,128,1024]{2,1,0:T(8,128)(2,1)} %param.12) | copy-start | bytes 786436

commit v3 on v2

--- a/solution.py
+++ b/solution.py
@@ -88,8 +88,8 @@
 
 
 def fused_kernel(
-    scale, query_hbm, key_hbm, value_hbm, grad_hbm, taps, first_both, last_all, twist_ref, mats, landed, gathered,
-    inputs, packed, arrived, back, signals, filters, filter_spectra, spectra, results, sums, pair_sums, parts,
+    scale, query_hbm, key_hbm, value_hbm, grad_hbm, taps_hbm, first_hbm, last_hbm, twist_hbm, mats_hbm, landed,
+    inputs, taps, first_both, last_all, twist_ref, mats, packed, arrived, back, signals, filters, filter_spectra, spectra, results, sums, pair_sums, parts,
     load_sem, out_send, out_recv, back_send, back_recv, own_sem, pair_send, pair_recv, part_send, part_recv,
 ):
     z_hi, core, ctx = place()
@@ -99,6 +99,8 @@
         pltpu.make_async_copy(ref, inputs.at[i], load_sem.at[i])
         for i, ref in enumerate((key_hbm, value_hbm, grad_hbm, query_hbm))
     ]
+    later = ((taps_hbm, taps), (first_hbm, first_both), (last_hbm, last_all), (twist_hbm, twist_ref), (mats_hbm, mats))
+    loads += [pltpu.make_async_copy(ref, held, load_sem.at[4 + i]) for i, (ref, held) in enumerate(later)]
     for load in loads:
         load.start()
 
@@ -147,7 +149,7 @@
     def part_copy(half, there, slot):
         return pltpu.make_async_remote_copy(
             src_ref=parts.at[half, there],
-            dst_ref=gathered.at[half, slot],
+            dst_ref=landed.at[N1 + half * 4 + slot],
             send_sem=part_send.at[half, there],
             recv_sem=part_recv.at[half, slot],
             device_id=(there * 2 + core, ctx),
@@ -161,7 +163,7 @@
 
         lax.fori_loop(0, 31, run, 0)
 
-    for load in loads:
+    for load in loads[:4]:
         load.wait()
     x, z_lo = ctx // 8, (ctx // 4) % 2
     for order, (dx, dz) in enumerate(((2, 1), (2, 0), (1, 1), (3, 1), (1, 0), (3, 0), (0, 1), (0, 0))):
@@ -181,10 +183,18 @@
     own = [
         pltpu.make_async_copy(packed.at[ctx, half], arrived.at[ctx, half], own_sem.at[half]) for half in range(2)
     ]
+    keep = [
+        pltpu.make_async_copy(back.at[ctx, half], landed.at[ctx, half], own_sem.at[2 + half]) for half in range(2)
+    ] + [
+        pltpu.make_async_copy(parts.at[half, z_hi], landed.at[N1 + half * 4 + z_hi], own_sem.at[4 + half])
+        for half in range(2)
+    ]
     own[0].start()
     own[1].start()
     steps(lambda there: out_copy(1, there, ctx).start())
 
+    for load in loads[4:]:
+        load.wait()
     twist = (twist_ref[0], twist_ref[1])
     for n1 in range(N1):
         filters[32 * n1 : 32 * n1 + 32] = taps[:, N2 * n1 : N2 * n1 + N2]
@@ -265,15 +275,17 @@
         for z in range(4):
             pair_copy(half, z).start()
         steps(lambda there: back_copy(half, there, ctx).start())
-        landed[ctx, half] = back[ctx, half]
+        keep[half].start()
         for z in range(4):
             pair_copy(half, z).wait()
             mine = sums[half, pl.ds(pl.multiple_of((z * 2 + core) * 64, 64), 64)]
-            parts[half, z] = (mine + pair_sums[half, z]).astype(BF16)
+            parts[half, z] = (mine + pair_sums[half, z]).astype(BF16).reshape(2, 2, HALF, N2)
         for away in (2, 1, 3):
             part_copy(half, (z_hi + away) % 4, z_hi).start()
-        gathered[half, z_hi] = parts[half, z_hi]
-
+        keep[2 + half].start()
+
+    for copy in keep:
+        copy.wait()
     for half in range(2):
         steps(lambda there: out_copy(half, there, there).wait_send())
         steps(lambda there: back_copy(half, there, there).wait())
@@ -282,7 +294,7 @@
             part_copy(half, there, there).wait()
 
 
-def gate_kernel(landed, gathered, query, key, value, grad, query_grad, key_grad, value_grad, taps_grad):
+def gate_kernel(landed, query, key, value, grad, query_grad, key_grad, value_grad, taps_grad):
     for block in range(8):
         lanes = slice(128 * block, 128 * block + 128)
         devices = slice(4 * block, 4 * block + 4)
@@ -292,9 +304,9 @@
         key_grad[:, lanes] = (inner * value[:, lanes].astype(F32)).astype(BF16)
         value_grad[:, lanes] = (inner * key[:, lanes].astype(F32)).astype(BF16)
     for half in range(2):
-        total = gathered[half, 0].astype(F32)
+        total = landed[N1 + 4 * half].reshape(4 * HALF, N2).astype(F32)
         for z in range(1, 4):
-            total = total + gathered[half, z].astype(F32)
+            total = total + landed[N1 + 4 * half + z].reshape(4 * HALF, N2).astype(F32)
         for n1 in range(4):
             taps_grad[16 * half : 16 * half + 16, N2 * n1 : N2 * n1 + N2] = total[16 * n1 : 16 * n1 + 16]
 
@@ -304,17 +316,22 @@
     query, key, value, grad = (a.reshape(rows, -1) for a in (query_proj, key_proj, value_proj, out_grad))
     vmem = pl.BlockSpec(memory_space=pltpu.VMEM)
     anywhere = pl.BlockSpec(memory_space=pl.ANY)
-    limit = 40 * 1024 * 1024
+    limit = 62 * 1024 * 1024
     slabs = (N1, 2, 2, HALF, N2)
     scale = 1.0 / math.sqrt(lax.axis_size("dp") * LENGTH)
     dma = pltpu.SemaphoreType.DMA
-    landed, gathered = pl.pallas_call(
+    landed = pl.pallas_call(
         functools.partial(fused_kernel, scale),
-        out_shape=(jax.ShapeDtypeStruct(slabs, BF16), jax.ShapeDtypeStruct((2, 4, 64, N2), BF16)),
-        in_specs=[anywhere] * 4 + [vmem] * 5,
-        out_specs=(vmem, vmem),
+        out_shape=jax.ShapeDtypeStruct((N1 + 8,) + slabs[1:], BF16),
+        in_specs=[anywhere] * 9,
+        out_specs=anywhere,
         scratch_shapes=[
             pltpu.VMEM((4, rows, query.shape[1]), BF16),
+            pltpu.VMEM((2 * HALF, LENGTH), F32),
+            pltpu.VMEM((2 * N1, 2 * N1), BF16),
+            pltpu.VMEM((N1, 6 * N1), BF16),
+            pltpu.VMEM((2, N1, N2), F32),
+            pltpu.VMEM((4, 2 * N2, 2 * N2), BF16),
             pltpu.VMEM(slabs, BF16),
             pltpu.VMEM(slabs, BF16),
             pltpu.VMEM(slabs, BF16),
@@ -325,13 +342,13 @@
             pltpu.VMEM((3 * GROUP * N1, 2 * N2), F32),
             pltpu.VMEM((2, N1 * HALF, N2), F32),
             pltpu.VMEM((2, 4, 64, N2), F32),
-            pltpu.VMEM((2, 4, 64, N2), BF16),
-            dma((4,)),
+            pltpu.VMEM((2, 4, 2, 2, HALF, N2), BF16),
+            dma((9,)),
             dma((2, 32)),
             dma((2, 32)),
             dma((2, 32)),
             dma((2, 32)),
-            dma((2,)),
+            dma((6,)),
             dma((2, 4)),
             dma((2, 4)),
             dma((2, 4)),
@@ -344,11 +361,11 @@
     outs = pl.pallas_call(
         gate_kernel,
         out_shape=(flat, flat, flat, jax.ShapeDtypeStruct((2 * HALF, 4 * N2), F32)),
-        in_specs=[vmem] * 6,
+        in_specs=[vmem] * 5,
         out_specs=(vmem,) * 4,
         compiler_params=pltpu.CompilerParams(vmem_limit_bytes=48 * 1024 * 1024),
         name="gate",
-    )(landed, gathered, query, key, value, grad)
+    )(landed, query, key, value, grad)
     return tuple(o.reshape(query_proj.shape) for o in outs[:3]) + (outs[3].T,)
 
 

time: 49.6 us -> 42.4 us (0.85)
  local copies, waits for them, and re-layouts: 8.08 us -> 1.1 us
    unnamed x26 -> x10, local copies, waits for them, and re-layouts: 8.08 us -> 1.1 us
where the time goes in v3:
time: 42.4 us; the launch traced here: 42.3 us
  Pallas kernels  40.5 us (96%)
  local copies, waits for them, and re-layouts  1.1 us (3%)
  between operations  0.71 us (2%)
    pallas_call x1, Pallas kernels, on_device(): pl.pallas_call(functools.partial(fused_kernel, scale), out_shape=jax.Shap...  39.3 us
    pallas_call x1, Pallas kernels, on_device(): pl.pallas_call(gate_kernel, out_shape=(flat, flat, flat, jax.ShapeDtypeSt...  1.15 us
    unnamed x10, local copies, waits for them, and re-layouts  1.1 us

profile of v3, /device:TPU:1, one launch (start us, length us, event | category | flops | bytes accessed | tf_op | source)
XLA Modules:
  0.0 42.3 jit_solution(12574903808866510062)
XLA Ops:
  0.6 0.0 copy-start.1
  0.6 0.0 copy-start.2
  0.7 0.0 copy-start.3
  0.7 0.0 copy-start.4
  0.7 39.3 %exchange_convolve.1.landed = bf16[40,2,2,16,128]{4,3,2,1,0:T(8,128)(2,1)} custom-call(bf16[128,1024]{1,0:T(8,128)(2,1)} %bitcast.9, bf16[128,1024]{1,0:T(8,128)(2,1)} %bitcast.11, bf16[128,1024]{1,0:T(8,128)(2,1)} %bitcast.13, bf16[128,1024]{1,0:T(8,128)(2,1)} %bitcast.15, f32[32,4096]{1,0:T(8,128)} %bitcast.17, bf16[64,64]{1,0:T(8,128)(2,1)} %constant.8.clone.first_hbm, ...), custom_call_target="tpu_custom_call" | custom-call | tf_op jit(solution)/shard_map/exchange_convolve/pallas_call | solution.py:323
  40.0 0.0 copy-done.1
  40.0 0.0 copy-done.2
  40.0 0.0 copy-done.3
  40.0 0.0 copy-done.4
  40.0 0.0 copy-start
  40.0 1.1 %copy-done = bf16[40,2,2,16,128]{4,3,2,1,0:T(8,128)(2,1)S(1)} copy-done((bf16[40,2,2,16,128]{4,3,2,1,0:T(8,128)(2,1)S(1)}, bf16[40,2,2,16,128]{4,3,2,1,0:T(8,128)(2,1)}, u32[]{:S(2)}) %copy-start) | copy-done | bytes 655384
  41.1 1.1 %gate.1 = (bf16[128,1024]{1,0:T(8,128)(2,1)}, bf16[128,1024]{1,0:T(8,128)(2,1)}, bf16[128,1024]{1,0:T(8,128)(2,1)}, f32[32,512]{1,0:T(8,128)}) custom-call(bf16[40,2,2,16,128]{4,3,2,1,0:T(8,128)(2,1)S(1)} %copy-done, bf16[128,1024]{1,0:T(8,128)(2,1)S(1)} %bitcast.10, bf16[128,1024]{1,0:T(8,128)(2,1)S(1)} %bitcast.12, bf16[128,1024]{1,0:T(8,128)(2,1)S(1)} %bitcast.14, ...), custom_call_target="tpu_custom_call" | custom-call | tf_op jit(solution)/shard_map/gate/pallas_call | solution.py:361
Async XLA Ops:
  0.6 39.4 %copy-start.1 = (bf16[1,128,1024]{2,1,0:T(8,128)(2,1)S(1)}, bf16[1,128,1024]{2,1,0:T(8,128)(2,1)}, u32[]{:S(2)}) copy-start(bf16[1,128,1024]{2,1,0:T(8,128)(2,1)} %param.9) | copy-start | bytes 786436
  0.6 39.4 %copy-start.2 = (bf16[1,128,1024]{2,1,0:T(8,128)(2,1)S(1)}, bf16[1,128,1024]{2,1,0:T(8,128)(2,1)}, u32[]{:S(2)}) copy-start(bf16[1,128,1024]{2,1,0:T(8,128)(2,1)} %param.10) | copy-start | bytes 786436
  0.7 39.4 %copy-start.3 = (bf16[1,128,1024]{2,1,0:T(8,128)(2,1)S(1)}, bf16[1,128,1024]{2,1,0:T(8,128)(2,1)}, u32[]{:S(2)}) copy-start(bf16[1,128,1024]{2,1,0:T(8,128)(2,1)} %param.11) | copy-start | bytes 786436
  0.7 39.4 %copy-start.4 = (bf16[1,128,1024]{2,1,0:T(8,128)(2,1)S(1)}, bf16[1,128,1024]{2,1,0:T(8,128)(2,1)}, u32[]{:S(2)}) copy-start(bf16[1,128,1024]{2,1,0:T(8,128)(2,1)} %param.12) | copy-start | bytes 786436
  40.0 1.1 %copy-start = (bf16[40,2,2,16,128]{4,3,2,1,0:T(8,128)(2,1)S(1)}, bf16[40,2,2,16,128]{4,3,2,1,0:T(8,128)(2,1)}, u32[]{:S(2)}) copy-start(bf16[40,2,2,16,128]{4,3,2,1,0:T(8,128)(2,1)} %exchange_convolve.1.landed) | copy-start | bytes 1966084

commit v4 on v3

--- a/solution.py
+++ b/solution.py
@@ -44,7 +44,11 @@
     cos, sin = np.cos(inner), np.sin(inner)
     forward = np.block([[cos, -sin], [sin, cos]])
     inverse = np.block([[cos, sin], [-sin, cos]])
-    stacked = np.stack(high_low(forward) + high_low(inverse))
+    stacked = []
+    for matrix in (forward, inverse):
+        high, low = high_low(matrix)
+        stacked.append(np.concatenate([high, high, low], axis=0))
+    stacked = np.stack(stacked)
     return first_both, last_all, twist, stacked
 
 
@@ -54,13 +58,10 @@
     return dp // 2, dp % 2, ctx
 
 
-def gray(j):
-    return j + (j // 2) * (1 - 2 * (j % 2))
-
-
-def peer_of(step, ctx):
-    x, z, y = ctx // 8, (ctx // 4) % 2, ctx % 4
-    return ((x + gray(step // 8)) % 4) * 8 + ((z + step % 2) % 2) * 4 + (y + gray((step // 2) % 4)) % 4
+OFFSETS = sorted(
+    ((dx, dz, dy) for dx in range(4) for dz in range(2) for dy in range(4) if dx or dz or dy),
+    key=lambda o: -(min(o[0], 4 - o[0]) + o[1] + min(o[2], 4 - o[2])),
+)
 
 
 def split(value):
@@ -72,9 +73,9 @@
     return lax.dot_general(left, right, (((1,), (0,)), ((), ())), preferred_element_type=F32)
 
 
-def middle(value, high, low):
-    value_high, value_low = split(value)
-    return dot(value_high, high) + dot(value_low, high) + dot(value_high, low)
+def middle(value, stacked):
+    high, low = split(value)
+    return dot(jnp.concatenate([high, low, high], axis=1), stacked[...])
 
 
 def twisted(value, twist):
@@ -106,35 +107,39 @@
 
     barrier = pltpu.get_barrier_semaphore()
 
-    def greet(step, carry):
-        pl.semaphore_signal(barrier, inc=1, device_id=(dp, peer_of(step, ctx)), device_id_type=MESH)
-        return carry
-
-    lax.fori_loop(1, 32, greet, 0)
+    xs = [((ctx // 8 + d) % 4) * 8 for d in range(4)]
+    zs = [((ctx // 4 + d) % 2) * 4 for d in range(2)]
+    ys = [(ctx + d) % 4 for d in range(4)]
+    partners = [xs[dx] + zs[dz] + ys[dy] for dx, dz, dy in OFFSETS]
+    for there in partners:
+        pl.semaphore_signal(barrier, inc=1, device_id=(dp, there), device_id_type=MESH)
     pl.semaphore_signal(barrier, inc=1, device_id=pair, device_id_type=MESH)
     for away in range(1, 4):
         there = ((z_hi + away) % 4) * 2 + core
         pl.semaphore_signal(barrier, inc=1, device_id=(there, ctx), device_id_type=MESH)
 
-    def out_copy(half, there, slot):
+    def out_copy(half, there):
         return pltpu.make_async_remote_copy(
-            src_ref=packed.at[there, half],
-            dst_ref=arrived.at[slot, half],
-            send_sem=out_send.at[half, there],
-            recv_sem=out_recv.at[half, slot],
+            src_ref=packed.at[half, there],
+            dst_ref=arrived.at[half, ctx],
+            send_sem=out_send.at[half],
+            recv_sem=out_recv.at[half],
             device_id=(dp, there),
             device_id_type=MESH,
         )
 
-    def back_copy(half, there, slot):
+    def back_copy(half, there):
         return pltpu.make_async_remote_copy(
-            src_ref=back.at[there, half],
-            dst_ref=landed.at[slot, half],
-            send_sem=back_send.at[half, there],
-            recv_sem=back_recv.at[half, slot],
+            src_ref=back.at[half, there],
+            dst_ref=landed.at[half * N1 + ctx],
+            send_sem=back_send.at[half],
+            recv_sem=back_recv.at[half],
             device_id=(dp, there),
             device_id_type=MESH,
         )
+
+    def wait_for(ref, sem):
+        pltpu.make_async_copy(ref, ref, sem).wait()
 
     def pair_copy(half, z):
         return pltpu.make_async_remote_copy(
@@ -149,49 +154,43 @@
     def part_copy(half, there, slot):
         return pltpu.make_async_remote_copy(
             src_ref=parts.at[half, there],
-            dst_ref=landed.at[N1 + half * 4 + slot],
+            dst_ref=landed.at[pl.ds(2 * N1 + (half * 4 + slot) * 2, 2)],
             send_sem=part_send.at[half, there],
             recv_sem=part_recv.at[half, slot],
             device_id=(there * 2 + core, ctx),
             device_id_type=MESH,
         )
 
-    def steps(body):
-        def run(step, carry):
-            body(peer_of(31 - step, ctx))
-            return carry
-
-        lax.fori_loop(0, 31, run, 0)
-
     for load in loads[:4]:
         load.wait()
-    x, z_lo = ctx // 8, (ctx // 4) % 2
     for order, (dx, dz) in enumerate(((2, 1), (2, 0), (1, 1), (3, 1), (1, 0), (3, 0), (0, 1), (0, 0))):
-        block = ((x + dx) % 4) * 2 + (z_lo + dz) % 2
-        lanes = pl.ds(pl.multiple_of(128 * block, 128), 128)
+        first = xs[dx] + zs[dz]
+        lanes = pl.ds(pl.multiple_of(first * 32, 128), 128)
         for array in range(2):
             gated = inputs[2 * array, :, lanes].astype(F32) * inputs[2 * array + 1, :, lanes].astype(F32)
             turned = gated.T.astype(BF16)
             for part in range(8):
-                packed[4 * block + part // 2, part % 2, array] = turned[16 * part : 16 * part + 16]
+                packed[part % 2, first + part // 2, array] = turned[16 * part : 16 * part + 16]
         if order == 0:
             pl.semaphore_wait(barrier, 35)
         for dy in (2, 1, 3, 0):
             if dx or dz or dy:
-                there = 4 * block + (ctx + dy) % 4
-                out_copy(0, there, ctx).start()
+                out_copy(0, first + ys[dy]).start()
     own = [
-        pltpu.make_async_copy(packed.at[ctx, half], arrived.at[ctx, half], own_sem.at[half]) for half in range(2)
+        pltpu.make_async_copy(packed.at[half, ctx], arrived.at[half, ctx], out_recv.at[half]) for half in range(2)
     ]
     keep = [
-        pltpu.make_async_copy(back.at[ctx, half], landed.at[ctx, half], own_sem.at[2 + half]) for half in range(2)
+        pltpu.make_async_copy(back.at[half, ctx], landed.at[half * N1 + ctx], back_recv.at[half]) for half in range(2)
     ] + [
-        pltpu.make_async_copy(parts.at[half, z_hi], landed.at[N1 + half * 4 + z_hi], own_sem.at[4 + half])
+        pltpu.make_async_copy(
+            parts.at[half, z_hi], landed.at[pl.ds(2 * N1 + (half * 4 + z_hi) * 2, 2)], own_sem.at[half]
+        )
         for half in range(2)
     ]
     own[0].start()
     own[1].start()
-    steps(lambda there: out_copy(1, there, ctx).start())
+    for there in partners:
+        out_copy(1, there).start()
 
     for load in loads[4:]:
         load.wait()
@@ -208,21 +207,20 @@
             out = dot(left, jnp.concatenate([high, high], axis=0)) + dot(left[:, :N1], low)
             forward += [twisted(out[:, :N2], twist), twisted(out[:, N2:], twist)]
         rows = pl.ds(pl.multiple_of(group * GROUP * N1, GROUP * N1), GROUP * N1)
-        filter_spectra[rows] = middle(jnp.concatenate(forward, axis=0), mats[0], mats[1])
+        filter_spectra[rows] = middle(jnp.concatenate(forward, axis=0), mats.at[0])
         return carry
 
     lax.fori_loop(0, 2 * HALF // GROUP, filter_work, 0)
 
     for half in range(2):
-        steps(lambda there: out_copy(half, there, there).wait_recv())
-        own[half].wait()
+        wait_for(arrived.at[half], out_recv.at[half])
 
         def unpack(n1, carry):
-            rows = arrived[n1, half].reshape(32, N2).astype(F32)
+            rows = arrived[half, n1].reshape(32, N2).astype(F32)
             signals[pl.ds(pl.multiple_of(n1 * 32, 32), 32)] = rows
             return carry
 
-        lax.fori_loop(0, N1, unpack, 0)
+        lax.fori_loop(0, N1, unpack, 0, unroll=8)
 
         def work(group, carry):
             forward = []
@@ -231,7 +229,7 @@
                 data = jnp.concatenate(rows, axis=1).astype(BF16)
                 out = dot(first_both[...], jnp.concatenate([data, data], axis=0))
                 forward += [twisted(out[:, :N2], twist), twisted(out[:, N2:], twist)]
-            spectra[...] = middle(jnp.concatenate(forward, axis=0), mats[0], mats[1])
+            spectra[...] = middle(jnp.concatenate(forward, axis=0), mats.at[0])
             inverse = []
             for item in range(GROUP):
                 start = (half * HALF + group * GROUP + item) * N1
@@ -244,7 +242,7 @@
                 inverse.append(jnp.concatenate([h_re * u_re - h_im * u_im, h_re * u_im + h_im * u_re], axis=1))
                 inverse.append(jnp.concatenate([m_re * h_re + m_im * h_im, m_im * h_re - m_re * h_im], axis=1))
                 inverse.append(jnp.concatenate([m_re * u_re + m_im * u_im, m_im * u_re - m_re * u_im], axis=1))
-            results[...] = middle(jnp.concatenate(inverse, axis=0), mats[2], mats[3])
+            results[...] = middle(jnp.concatenate(inverse, axis=0), mats.at[1])
 
             def finish(indices):
                 turned = [untwisted(results[N1 * i : N1 * i + N1], twist) for i in indices]
@@ -252,29 +250,34 @@
                 out = dot(last_all[...], jnp.concatenate([high, low, high], axis=0))
                 return out[:, :N2], out[:, N2:]
 
+            for item in range(0, GROUP, 2):
+                c = group * GROUP + item
+                first, second = finish((3 * item + 2, 3 * item + 5))
+                sums[half, pl.ds(c, N1, stride=HALF)] = first * scale
+                sums[half, pl.ds(c + 1, N1, stride=HALF)] = second * scale
+
+            @pl.when(group == HALF // GROUP - 1)
+            def _():
+                for z in range(4):
+                    pair_copy(half, z).start()
+
             for item in range(GROUP):
                 c = group * GROUP + item
                 conv, inner = finish((3 * item, 3 * item + 1))
                 signals[pl.ds(c, N1, stride=32)] = conv
                 signals[pl.ds(c + HALF, N1, stride=32)] = inner
-            for item in range(0, GROUP, 2):
-                c = group * GROUP + item
-                first, second = finish((3 * item + 2, 3 * item + 5))
-                sums[half, pl.ds(c, N1, stride=HALF)] = first * scale
-                sums[half, pl.ds(c + 1, N1, stride=HALF)] = second * scale
             return carry
 
         lax.fori_loop(0, HALF // GROUP, work, 0)
 
         def pack(n1, carry):
             rows = signals[pl.ds(pl.multiple_of(n1 * 32, 32), 32)].astype(BF16)
-            back[n1, half] = rows.reshape(2, 16, N2)
+            back[half, n1] = rows.reshape(2, 16, N2)
             return carry
 
-        lax.fori_loop(0, N1, pack, 0)
-        for z in range(4):
-            pair_copy(half, z).start()
-        steps(lambda there: back_copy(half, there, ctx).start())
+        lax.fori_loop(0, N1, pack, 0, unroll=8)
+        for there in partners:
+            back_copy(half, there).start()
         keep[half].start()
         for z in range(4):
             pair_copy(half, z).wait()
@@ -284,11 +287,11 @@
             part_copy(half, (z_hi + away) % 4, z_hi).start()
         keep[2 + half].start()
 
-    for copy in keep:
-        copy.wait()
     for half in range(2):
-        steps(lambda there: out_copy(half, there, there).wait_send())
-        steps(lambda there: back_copy(half, there, there).wait())
+        wait_for(packed.at[half, pl.ds(0, N1 - 1)], out_send.at[half])
+        wait_for(back.at[half, pl.ds(0, N1 - 1)], back_send.at[half])
+        wait_for(landed.at[pl.ds(half * N1, N1)], back_recv.at[half])
+        keep[2 + half].wait()
         for away in (2, 1, 3):
             there = (z_hi + away) % 4
             part_copy(half, there, there).wait()
@@ -297,16 +300,17 @@
 def gate_kernel(landed, query, key, value, grad, query_grad, key_grad, value_grad, taps_grad):
     for block in range(8):
         lanes = slice(128 * block, 128 * block + 128)
-        devices = slice(4 * block, 4 * block + 4)
-        conv = landed[devices, :, 0].reshape(128, N2).astype(F32).T
-        inner = landed[devices, :, 1].reshape(128, N2).astype(F32).T
+        slots = [half * N1 + 4 * block + device for device in range(4) for half in range(2)]
+        conv = jnp.concatenate([landed[slot, 0] for slot in slots], axis=0).astype(F32).T
+        inner = jnp.concatenate([landed[slot, 1] for slot in slots], axis=0).astype(F32).T
         query_grad[:, lanes] = (conv * grad[:, lanes].astype(F32)).astype(BF16)
         key_grad[:, lanes] = (inner * value[:, lanes].astype(F32)).astype(BF16)
         value_grad[:, lanes] = (inner * key[:, lanes].astype(F32)).astype(BF16)
     for half in range(2):
-        total = landed[N1 + 4 * half].reshape(4 * HALF, N2).astype(F32)
-        for z in range(1, 4):
-            total = total + landed[N1 + 4 * half + z].reshape(4 * HALF, N2).astype(F32)
+        pieces = [2 * N1 + (4 * half + z) * 2 for z in range(4)]
+        total = landed[pieces[0] : pieces[0] + 2].reshape(4 * HALF, N2).astype(F32)
+        for piece in pieces[1:]:
+            total = total + landed[piece : piece + 2].reshape(4 * HALF, N2).astype(F32)
         for n1 in range(4):
             taps_grad[16 * half : 16 * half + 16, N2 * n1 : N2 * n1 + N2] = total[16 * n1 : 16 * n1 + 16]
 
@@ -317,12 +321,12 @@
     vmem = pl.BlockSpec(memory_space=pltpu.VMEM)
     anywhere = pl.BlockSpec(memory_space=pl.ANY)
     limit = 62 * 1024 * 1024
-    slabs = (N1, 2, 2, HALF, N2)
+    slabs = (2, N1, 2, HALF, N2)
     scale = 1.0 / math.sqrt(lax.axis_size("dp") * LENGTH)
     dma = pltpu.SemaphoreType.DMA
     landed = pl.pallas_call(
         functools.partial(fused_kernel, scale),
-        out_shape=jax.ShapeDtypeStruct((N1 + 8,) + slabs[1:], BF16),
+        out_shape=jax.ShapeDtypeStruct((2 * N1 + 16, 2, HALF, N2), BF16),
         in_specs=[anywhere] * 9,
         out_specs=anywhere,
         scratch_shapes=[
@@ -331,7 +335,7 @@
             pltpu.VMEM((2 * N1, 2 * N1), BF16),
             pltpu.VMEM((N1, 6 * N1), BF16),
             pltpu.VMEM((2, N1, N2), F32),
-            pltpu.VMEM((4, 2 * N2, 2 * N2), BF16),
+            pltpu.VMEM((2, 6 * N2, 2 * N2), BF16),
             pltpu.VMEM(slabs, BF16),
             pltpu.VMEM(slabs, BF16),
             pltpu.VMEM(slabs, BF16),
@@ -344,11 +348,11 @@
             pltpu.VMEM((2, 4, 64, N2), F32),
             pltpu.VMEM((2, 4, 2, 2, HALF, N2), BF16),
             dma((9,)),
-            dma((2, 32)),
-            dma((2, 32)),
-            dma((2, 32)),
-            dma((2, 32)),
-            dma((6,)),
+            dma((2,)),
+            dma((2,)),
+            dma((2,)),
+            dma((2,)),
+            dma((2,)),
             dma((2, 4)),
             dma((2, 4)),
             dma((2, 4)),

time: 42.4 us -> 37.5 us (0.88)
  Pallas kernels: 40.5 us -> 35.5 us
    pallas_call x1, Pallas kernels: 39.3 us -> 34.4 us  [on_device(): pl.pallas_call(functools.partial(fused_kernel, scale), out_shape=jax.Shap...]
where the time goes in v4:
time: 37.5 us; the launch traced here: 37.3 us
  Pallas kernels  35.5 us (95%)
  local copies, waits for them, and re-layouts  1.1 us (3%)
  between operations  0.71 us (2%)
    pallas_call x1, Pallas kernels, on_device(): pl.pallas_call(functools.partial(fused_kernel, scale), out_shape=jax.Shap...  34.4 us
    pallas_call x1, Pallas kernels, on_device(): pl.pallas_call(gate_kernel, out_shape=(flat, flat, flat, jax.ShapeDtypeSt...  1.15 us
    unnamed x10, local copies, waits for them, and re-layouts  1.1 us

profile of v4, /device:TPU:1, one launch (start us, length us, event | category | flops | bytes accessed | tf_op | source)
XLA Modules:
  0.0 37.3 jit_solution(18307700052747758919)
XLA Ops:
  0.6 0.0 copy-start.1
  0.6 0.0 copy-start.2
  0.7 0.0 copy-start.3
  0.7 0.0 copy-start.4
  0.7 34.4 %exchange_convolve.1.landed = bf16[80,2,16,128]{3,2,1,0:T(8,128)(2,1)} custom-call(bf16[128,1024]{1,0:T(8,128)(2,1)} %bitcast.9, bf16[128,1024]{1,0:T(8,128)(2,1)} %bitcast.11, bf16[128,1024]{1,0:T(8,128)(2,1)} %bitcast.13, bf16[128,1024]{1,0:T(8,128)(2,1)} %bitcast.15, f32[32,4096]{1,0:T(8,128)} %bitcast.17, bf16[64,64]{1,0:T(8,128)(2,1)} %constant.8.clone.first_hbm, ...), custom_call_target="tpu_custom_call" | custom-call | tf_op jit(solution)/shard_map/exchange_convolve/pallas_call | solution.py:327
  35.0 0.0 copy-done.1
  35.1 0.0 copy-done.2
  35.1 0.0 copy-done.3
  35.1 0.0 copy-done.4
  35.1 0.0 copy-start
  35.1 1.1 %copy-done = bf16[80,2,16,128]{3,2,1,0:T(8,128)(2,1)S(1)} copy-done((bf16[80,2,16,128]{3,2,1,0:T(8,128)(2,1)S(1)}, bf16[80,2,16,128]{3,2,1,0:T(8,128)(2,1)}, u32[]{:S(2)}) %copy-start) | copy-done | bytes 655384
  36.2 1.2 %gate.1 = (bf16[128,1024]{1,0:T(8,128)(2,1)}, bf16[128,1024]{1,0:T(8,128)(2,1)}, bf16[128,1024]{1,0:T(8,128)(2,1)}, f32[32,512]{1,0:T(8,128)}) custom-call(bf16[80,2,16,128]{3,2,1,0:T(8,128)(2,1)S(1)} %copy-done, bf16[128,1024]{1,0:T(8,128)(2,1)S(1)} %bitcast.10, bf16[128,1024]{1,0:T(8,128)(2,1)S(1)} %bitcast.12, bf16[128,1024]{1,0:T(8,128)(2,1)S(1)} %bitcast.14, ...), custom_call_target="tpu_custom_call" | custom-call | tf_op jit(solution)/shard_map/gate/pallas_call | solution.py:365
Async XLA Ops:
  0.6 34.4 %copy-start.1 = (bf16[1,128,1024]{2,1,0:T(8,128)(2,1)S(1)}, bf16[1,128,1024]{2,1,0:T(8,128)(2,1)}, u32[]{:S(2)}) copy-start(bf16[1,128,1024]{2,1,0:T(8,128)(2,1)} %param.9) | copy-start | bytes 786436
  0.6 34.4 %copy-start.2 = (bf16[1,128,1024]{2,1,0:T(8,128)(2,1)S(1)}, bf16[1,128,1024]{2,1,0:T(8,128)(2,1)}, u32[]{:S(2)}) copy-start(bf16[1,128,1024]{2,1,0:T(8,128)(2,1)} %param.10) | copy-start | bytes 786436
  0.7 34.4 %copy-start.3 = (bf16[1,128,1024]{2,1,0:T(8,128)(2,1)S(1)}, bf16[1,128,1024]{2,1,0:T(8,128)(2,1)}, u32[]{:S(2)}) copy-start(bf16[1,128,1024]{2,1,0:T(8,128)(2,1)} %param.11) | copy-start | bytes 786436
  0.7 34.4 %copy-start.4 = (bf16[1,128,1024]{2,1,0:T(8,128)(2,1)S(1)}, bf16[1,128,1024]{2,1,0:T(8,128)(2,1)}, u32[]{:S(2)}) copy-start(bf16[1,128,1024]{2,1,0:T(8,128)(2,1)} %param.12) | copy-start | bytes 786436
  35.1 1.1 %copy-start = (bf16[80,2,16,128]{3,2,1,0:T(8,128)(2,1)S(1)}, bf16[80,2,16,128]{3,2,1,0:T(8,128)(2,1)}, u32[]{:S(2)}) copy-start(bf16[80,2,16,128]{3,2,1,0:T(8,128)(2,1)} %exchange_convolve.1.landed) | copy-start | bytes 1966084

commit v5 on v4

--- a/solution.py
+++ b/solution.py
@@ -168,7 +168,7 @@
         lanes = pl.ds(pl.multiple_of(first * 32, 128), 128)
         for array in range(2):
             gated = inputs[2 * array, :, lanes].astype(F32) * inputs[2 * array + 1, :, lanes].astype(F32)
-            turned = gated.T.astype(BF16)
+            turned = gated.astype(BF16).T
             for part in range(8):
                 packed[part % 2, first + part // 2, array] = turned[16 * part : 16 * part + 16]
         if order == 0:
@@ -212,73 +212,7 @@
 
     lax.fori_loop(0, 2 * HALF // GROUP, filter_work, 0)
 
-    for half in range(2):
-        wait_for(arrived.at[half], out_recv.at[half])
-
-        def unpack(n1, carry):
-            rows = arrived[half, n1].reshape(32, N2).astype(F32)
-            signals[pl.ds(pl.multiple_of(n1 * 32, 32), 32)] = rows
-            return carry
-
-        lax.fori_loop(0, N1, unpack, 0, unroll=8)
-
-        def work(group, carry):
-            forward = []
-            for item in range(GROUP):
-                rows = [signals[pl.ds(group * GROUP + item + HALF * i, N1, stride=32)] for i in range(2)]
-                data = jnp.concatenate(rows, axis=1).astype(BF16)
-                out = dot(first_both[...], jnp.concatenate([data, data], axis=0))
-                forward += [twisted(out[:, :N2], twist), twisted(out[:, N2:], twist)]
-            spectra[...] = middle(jnp.concatenate(forward, axis=0), mats.at[0])
-            inverse = []
-            for item in range(GROUP):
-                start = (half * HALF + group * GROUP + item) * N1
-                h = filter_spectra[pl.ds(pl.multiple_of(start, N1), N1)]
-                h_re, h_im = h[:, :N2], h[:, N2:]
-                u = spectra[2 * item * N1 : (2 * item + 1) * N1]
-                u_re, u_im = u[:, :N2], u[:, N2:]
-                m = spectra[(2 * item + 1) * N1 : (2 * item + 2) * N1]
-                m_re, m_im = m[:, :N2], m[:, N2:]
-                inverse.append(jnp.concatenate([h_re * u_re - h_im * u_im, h_re * u_im + h_im * u_re], axis=1))
-                inverse.append(jnp.concatenate([m_re * h_re + m_im * h_im, m_im * h_re - m_re * h_im], axis=1))
-                inverse.append(jnp.concatenate([m_re * u_re + m_im * u_im, m_im * u_re - m_re * u_im], axis=1))
-            results[...] = middle(jnp.concatenate(inverse, axis=0), mats.at[1])
-
-            def finish(indices):
-                turned = [untwisted(results[N1 * i : N1 * i + N1], twist) for i in indices]
-                high, low = split(jnp.concatenate(turned, axis=1))
-                out = dot(last_all[...], jnp.concatenate([high, low, high], axis=0))
-                return out[:, :N2], out[:, N2:]
-
-            for item in range(0, GROUP, 2):
-                c = group * GROUP + item
-                first, second = finish((3 * item + 2, 3 * item + 5))
-                sums[half, pl.ds(c, N1, stride=HALF)] = first * scale
-                sums[half, pl.ds(c + 1, N1, stride=HALF)] = second * scale
-
-            @pl.when(group == HALF // GROUP - 1)
-            def _():
-                for z in range(4):
-                    pair_copy(half, z).start()
-
-            for item in range(GROUP):
-                c = group * GROUP + item
-                conv, inner = finish((3 * item, 3 * item + 1))
-                signals[pl.ds(c, N1, stride=32)] = conv
-                signals[pl.ds(c + HALF, N1, stride=32)] = inner
-            return carry
-
-        lax.fori_loop(0, HALF // GROUP, work, 0)
-
-        def pack(n1, carry):
-            rows = signals[pl.ds(pl.multiple_of(n1 * 32, 32), 32)].astype(BF16)
-            back[half, n1] = rows.reshape(2, 16, N2)
-            return carry
-
-        lax.fori_loop(0, N1, pack, 0, unroll=8)
-        for there in partners:
-            back_copy(half, there).start()
-        keep[half].start()
+    def sum_parts(half):
         for z in range(4):
             pair_copy(half, z).wait()
             mine = sums[half, pl.ds(pl.multiple_of((z * 2 + core) * 64, 64), 64)]
@@ -286,6 +220,86 @@
         for away in (2, 1, 3):
             part_copy(half, (z_hi + away) % 4, z_hi).start()
         keep[2 + half].start()
+
+    for half in range(2):
+        wait_for(arrived.at[half], out_recv.at[half])
+
+        def unpack(n1, carry):
+            rows = arrived[half, n1].reshape(32, N2).astype(F32)
+            signals[pl.ds(pl.multiple_of(n1 * 32, 32), 32)] = rows
+            return carry
+
+        lax.fori_loop(0, N1, unpack, 0, unroll=8)
+
+        def spectrum(index):
+            block = spectra[pl.ds(pl.multiple_of(index * N1, N1), N1)]
+            return block[:, :N2], block[:, N2:]
+
+        def finish(indices):
+            turned = [untwisted(results[N1 * i : N1 * i + N1], twist) for i in indices]
+            high, low = split(jnp.concatenate(turned, axis=1))
+            out = dot(last_all[...], jnp.concatenate([high, low, high], axis=0))
+            return out[:, :N2], out[:, N2:]
+
+        def taps_work(group, carry):
+            forward = []
+            for item in range(GROUP):
+                rows = [signals[pl.ds(group * GROUP + item + HALF * i, N1, stride=32)] for i in range(2)]
+                data = jnp.concatenate(rows, axis=1).astype(BF16)
+                out = dot(first_both[...], jnp.concatenate([data, data], axis=0))
+                forward += [twisted(out[:, :N2], twist), twisted(out[:, N2:], twist)]
+            rows = pl.ds(pl.multiple_of(group * 2 * GROUP * N1, 2 * GROUP * N1), 2 * GROUP * N1)
+            spectra[rows] = middle(jnp.concatenate(forward, axis=0), mats.at[0])
+            inverse = []
+            for item in range(GROUP):
+                u_re, u_im = spectrum(2 * (group * GROUP + item))
+                m_re, m_im = spectrum(2 * (group * GROUP + item) + 1)
+                inverse.append(jnp.concatenate([m_re * u_re + m_im * u_im, m_im * u_re - m_re * u_im], axis=1))
+            results[: GROUP * N1] = middle(jnp.concatenate(inverse, axis=0), mats.at[1])
+            for item in range(0, GROUP, 2):
+                c = group * GROUP + item
+                first, second = finish((item, item + 1))
+                sums[half, pl.ds(c, N1, stride=HALF)] = first * scale
+                sums[half, pl.ds(c + 1, N1, stride=HALF)] = second * scale
+            return carry
+
+        lax.fori_loop(0, HALF // GROUP, taps_work, 0)
+        for z in range(4):
+            pair_copy(half, z).start()
+        if half == 1:
+            sum_parts(0)
+
+        def work(group, carry):
+            inverse = []
+            for item in range(GROUP):
+                start = (half * HALF + group * GROUP + item) * N1
+                h = filter_spectra[pl.ds(pl.multiple_of(start, N1), N1)]
+                h_re, h_im = h[:, :N2], h[:, N2:]
+                u_re, u_im = spectrum(2 * (group * GROUP + item))
+                m_re, m_im = spectrum(2 * (group * GROUP + item) + 1)
+                inverse.append(jnp.concatenate([h_re * u_re - h_im * u_im, h_re * u_im + h_im * u_re], axis=1))
+                inverse.append(jnp.concatenate([m_re * h_re + m_im * h_im, m_im * h_re - m_re * h_im], axis=1))
+            results[...] = middle(jnp.concatenate(inverse, axis=0), mats.at[1])
+            for item in range(GROUP):
+                c = group * GROUP + item
+                conv, inner = finish((2 * item, 2 * item + 1))
+                signals[pl.ds(c, N1, stride=32)] = conv
+                signals[pl.ds(c + HALF, N1, stride=32)] = inner
+            return carry
+
+        lax.fori_loop(0, HALF // GROUP, work, 0)
+
+        def pack(n1, carry):
+            rows = signals[pl.ds(pl.multiple_of(n1 * 32, 32), 32)].astype(BF16)
+            back[half, n1] = rows.reshape(2, 16, N2)
+            return carry
+
+        lax.fori_loop(0, N1, pack, 0, unroll=8)
+        if half == 1:
+            sum_parts(half)
+        for there in partners:
+            back_copy(half, there).start()
+        keep[half].start()
 
     for half in range(2):
         wait_for(packed.at[half, pl.ds(0, N1 - 1)], out_send.at[half])
@@ -342,8 +356,8 @@
             pltpu.VMEM((N1 * 2 * HALF, N2), F32),
             pltpu.VMEM((N1 * 2 * HALF, N2), F32),
             pltpu.VMEM((2 * HALF * N1, 2 * N2), F32),
+            pltpu.VMEM((2 * HALF * N1, 2 * N2), F32),
             pltpu.VMEM((2 * GROUP * N1, 2 * N2), F32),
-            pltpu.VMEM((3 * GROUP * N1, 2 * N2), F32),
             pltpu.VMEM((2, N1 * HALF, N2), F32),
             pltpu.VMEM((2, 4, 64, N2), F32),
             pltpu.VMEM((2, 4, 2, 2, HALF, N2), BF16),

time: 37.5 us -> 36.5 us (0.973)
  Pallas kernels: 35.5 us -> 34.5 us
    pallas_call x1, Pallas kernels: 34.4 us -> 33.4 us  [on_device(): pl.pallas_call(functools.partial(fused_kernel, scale), out_shape=jax.Shap...]
where the time goes in v5:
time: 36.5 us; the launch traced here: 36.3 us
  Pallas kernels  34.5 us (95%)
  local copies, waits for them, and re-layouts  1.1 us (3%)
  between operations  0.71 us (2%)
    pallas_call x1, Pallas kernels, on_device(): pl.pallas_call(functools.partial(fused_kernel, scale), out_shape=jax.Shap...  33.4 us
    pallas_call x1, Pallas kernels, on_device(): pl.pallas_call(gate_kernel, out_shape=(flat, flat, flat, jax.ShapeDtypeSt...  1.15 us
    unnamed x10, local copies, waits for them, and re-layouts  1.1 us

profile of v5, /device:TPU:1, one launch (start us, length us, event | category | flops | bytes accessed | tf_op | source)
XLA Modules:
  0.0 36.3 jit_solution(2115199430557481453)
XLA Ops:
  0.6 0.0 copy-start.1
  0.6 0.0 copy-start.2
  0.7 0.0 copy-start.3
  0.7 0.0 copy-start.4
  0.7 33.4 %exchange_convolve.1.landed = bf16[80,2,16,128]{3,2,1,0:T(8,128)(2,1)} custom-call(bf16[128,1024]{1,0:T(8,128)(2,1)} %bitcast.9, bf16[128,1024]{1,0:T(8,128)(2,1)} %bitcast.11, bf16[128,1024]{1,0:T(8,128)(2,1)} %bitcast.13, bf16[128,1024]{1,0:T(8,128)(2,1)} %bitcast.15, f32[32,4096]{1,0:T(8,128)} %bitcast.17, bf16[64,64]{1,0:T(8,128)(2,1)} %constant.8.clone.first_hbm, ...), custom_call_target="tpu_custom_call" | custom-call | tf_op jit(solution)/shard_map/exchange_convolve/pallas_call | solution.py:341
  34.1 0.0 copy-done.1
  34.1 0.0 copy-done.2
  34.1 0.0 copy-done.3
  34.1 0.0 copy-done.4
  34.1 0.0 copy-start
  34.1 1.1 %copy-done = bf16[80,2,16,128]{3,2,1,0:T(8,128)(2,1)S(1)} copy-done((bf16[80,2,16,128]{3,2,1,0:T(8,128)(2,1)S(1)}, bf16[80,2,16,128]{3,2,1,0:T(8,128)(2,1)}, u32[]{:S(2)}) %copy-start) | copy-done | bytes 655384
  35.2 1.2 %gate.1 = (bf16[128,1024]{1,0:T(8,128)(2,1)}, bf16[128,1024]{1,0:T(8,128)(2,1)}, bf16[128,1024]{1,0:T(8,128)(2,1)}, f32[32,512]{1,0:T(8,128)}) custom-call(bf16[80,2,16,128]{3,2,1,0:T(8,128)(2,1)S(1)} %copy-done, bf16[128,1024]{1,0:T(8,128)(2,1)S(1)} %bitcast.10, bf16[128,1024]{1,0:T(8,128)(2,1)S(1)} %bitcast.12, bf16[128,1024]{1,0:T(8,128)(2,1)S(1)} %bitcast.14, ...), custom_call_target="tpu_custom_call" | custom-call | tf_op jit(solution)/shard_map/gate/pallas_call | solution.py:379
Async XLA Ops:
  0.6 33.4 %copy-start.1 = (bf16[1,128,1024]{2,1,0:T(8,128)(2,1)S(1)}, bf16[1,128,1024]{2,1,0:T(8,128)(2,1)}, u32[]{:S(2)}) copy-start(bf16[1,128,1024]{2,1,0:T(8,128)(2,1)} %param.9) | copy-start | bytes 786436
  0.6 33.4 %copy-start.2 = (bf16[1,128,1024]{2,1,0:T(8,128)(2,1)S(1)}, bf16[1,128,1024]{2,1,0:T(8,128)(2,1)}, u32[]{:S(2)}) copy-start(bf16[1,128,1024]{2,1,0:T(8,128)(2,1)} %param.10) | copy-start | bytes 786436
  0.7 33.4 %copy-start.3 = (bf16[1,128,1024]{2,1,0:T(8,128)(2,1)S(1)}, bf16[1,128,1024]{2,1,0:T(8,128)(2,1)}, u32[]{:S(2)}) copy-start(bf16[1,128,1024]{2,1,0:T(8,128)(2,1)} %param.11) | copy-start | bytes 786436
  0.7 33.4 %copy-start.4 = (bf16[1,128,1024]{2,1,0:T(8,128)(2,1)S(1)}, bf16[1,128,1024]{2,1,0:T(8,128)(2,1)}, u32[]{:S(2)}) copy-start(bf16[1,128,1024]{2,1,0:T(8,128)(2,1)} %param.12) | copy-start | bytes 786436
  34.1 1.1 %copy-start = (bf16[80,2,16,128]{3,2,1,0:T(8,128)(2,1)S(1)}, bf16[80,2,16,128]{3,2,1,0:T(8,128)(2,1)}, u32[]{:S(2)}) copy-start(bf16[80,2,16,128]{3,2,1,0:T(8,128)(2,1)} %exchange_convolve.1.landed) | copy-start | bytes 1966084

commit v6 on v5

--- a/solution.py
+++ b/solution.py
@@ -17,7 +17,7 @@
 N1 = 32
 N2 = 128
 LENGTH = N1 * N2
-GROUP = 8
+GROUP = 16
 HALF = 16
 
 
@@ -163,19 +163,16 @@
 
     for load in loads[:4]:
         load.wait()
-    for order, (dx, dz) in enumerate(((2, 1), (2, 0), (1, 1), (3, 1), (1, 0), (3, 0), (0, 1), (0, 0))):
-        first = xs[dx] + zs[dz]
-        lanes = pl.ds(pl.multiple_of(first * 32, 128), 128)
+    for block in range(8):
+        lanes = slice(128 * block, 128 * block + 128)
         for array in range(2):
             gated = inputs[2 * array, :, lanes].astype(F32) * inputs[2 * array + 1, :, lanes].astype(F32)
             turned = gated.astype(BF16).T
             for part in range(8):
-                packed[part % 2, first + part // 2, array] = turned[16 * part : 16 * part + 16]
-        if order == 0:
-            pl.semaphore_wait(barrier, 35)
-        for dy in (2, 1, 3, 0):
-            if dx or dz or dy:
-                out_copy(0, first + ys[dy]).start()
+                packed[part % 2, 4 * block + part // 2, array] = turned[16 * part : 16 * part + 16]
+    pl.semaphore_wait(barrier, 35)
+    for there in partners:
+        out_copy(0, there).start()
     own = [
         pltpu.make_async_copy(packed.at[half, ctx], arrived.at[half, ctx], out_recv.at[half]) for half in range(2)
     ]
@@ -295,11 +292,11 @@
             return carry
 
         lax.fori_loop(0, N1, pack, 0, unroll=8)
-        if half == 1:
-            sum_parts(half)
         for there in partners:
             back_copy(half, there).start()
         keep[half].start()
+        if half == 1:
+            sum_parts(half)
 
     for half in range(2):
         wait_for(packed.at[half, pl.ds(0, N1 - 1)], out_send.at[half])

time: 36.5 us -> 33.5 us (0.918)
  Pallas kernels: 34.5 us -> 31.2 us
    pallas_call x1, Pallas kernels: 33.4 us -> 30.1 us  [on_device(): pl.pallas_call(functools.partial(fused_kernel, scale), out_shape=jax.Shap...]
where the time goes in v6:
time: 33.5 us; the launch traced here: 33 us
  Pallas kernels  31.2 us (93%)
  local copies, waits for them, and re-layouts  1.1 us (3%)
  between operations  0.71 us (2%)
    pallas_call x1, Pallas kernels, on_device(): pl.pallas_call(functools.partial(fused_kernel, scale), out_shape=jax.Shap...  30.1 us
    pallas_call x1, Pallas kernels, on_device(): pl.pallas_call(gate_kernel, out_shape=(flat, flat, flat, jax.ShapeDtypeSt...  1.15 us
    unnamed x10, local copies, waits for them, and re-layouts  1.1 us

profile of v6, /device:TPU:1, one launch (start us, length us, event | category | flops | bytes accessed | tf_op | source)
XLA Modules:
  0.0 33.0 jit_solution(6463949960685369890)
XLA Ops:
  0.6 0.0 copy-start.1
  0.6 0.0 copy-start.2
  0.7 0.0 copy-start.3
  0.7 0.0 copy-start.4
  0.7 30.1 %exchange_convolve.1.landed = bf16[80,2,16,128]{3,2,1,0:T(8,128)(2,1)} custom-call(bf16[128,1024]{1,0:T(8,128)(2,1)} %bitcast.9, bf16[128,1024]{1,0:T(8,128)(2,1)} %bitcast.11, bf16[128,1024]{1,0:T(8,128)(2,1)} %bitcast.13, bf16[128,1024]{1,0:T(8,128)(2,1)} %bitcast.15, f32[32,4096]{1,0:T(8,128)} %bitcast.17, bf16[64,64]{1,0:T(8,128)(2,1)} %constant.8.clone.first_hbm, ...), custom_call_target="tpu_custom_call" | custom-call | tf_op jit(solution)/shard_map/exchange_convolve/pallas_call | solution.py:338
  30.7 0.0 copy-done.1
  30.7 0.0 copy-done.2
  30.8 0.0 copy-done.3
  30.8 0.0 copy-done.4
  30.8 0.0 copy-start
  30.8 1.1 %copy-done = bf16[80,2,16,128]{3,2,1,0:T(8,128)(2,1)S(1)} copy-done((bf16[80,2,16,128]{3,2,1,0:T(8,128)(2,1)S(1)}, bf16[80,2,16,128]{3,2,1,0:T(8,128)(2,1)}, u32[]{:S(2)}) %copy-start) | copy-done | bytes 655384
  31.9 1.2 %gate.1 = (bf16[128,1024]{1,0:T(8,128)(2,1)}, bf16[128,1024]{1,0:T(8,128)(2,1)}, bf16[128,1024]{1,0:T(8,128)(2,1)}, f32[32,512]{1,0:T(8,128)}) custom-call(bf16[80,2,16,128]{3,2,1,0:T(8,128)(2,1)S(1)} %copy-done, bf16[128,1024]{1,0:T(8,128)(2,1)S(1)} %bitcast.10, bf16[128,1024]{1,0:T(8,128)(2,1)S(1)} %bitcast.12, bf16[128,1024]{1,0:T(8,128)(2,1)S(1)} %bitcast.14, ...), custom_call_target="tpu_custom_call" | custom-call | tf_op jit(solution)/shard_map/gate/pallas_call | solution.py:376
Async XLA Ops:
  0.6 30.1 %copy-start.1 = (bf16[1,128,1024]{2,1,0:T(8,128)(2,1)S(1)}, bf16[1,128,1024]{2,1,0:T(8,128)(2,1)}, u32[]{:S(2)}) copy-start(bf16[1,128,1024]{2,1,0:T(8,128)(2,1)} %param.9) | copy-start | bytes 786436
  0.6 30.1 %copy-start.2 = (bf16[1,128,1024]{2,1,0:T(8,128)(2,1)S(1)}, bf16[1,128,1024]{2,1,0:T(8,128)(2,1)}, u32[]{:S(2)}) copy-start(bf16[1,128,1024]{2,1,0:T(8,128)(2,1)} %param.10) | copy-start | bytes 786436
  0.7 30.1 %copy-start.3 = (bf16[1,128,1024]{2,1,0:T(8,128)(2,1)S(1)}, bf16[1,128,1024]{2,1,0:T(8,128)(2,1)}, u32[]{:S(2)}) copy-start(bf16[1,128,1024]{2,1,0:T(8,128)(2,1)} %param.11) | copy-start | bytes 786436
  0.7 30.1 %copy-start.4 = (bf16[1,128,1024]{2,1,0:T(8,128)(2,1)S(1)}, bf16[1,128,1024]{2,1,0:T(8,128)(2,1)}, u32[]{:S(2)}) copy-start(bf16[1,128,1024]{2,1,0:T(8,128)(2,1)} %param.12) | copy-start | bytes 786436
  30.8 1.1 %copy-start = (bf16[80,2,16,128]{3,2,1,0:T(8,128)(2,1)S(1)}, bf16[80,2,16,128]{3,2,1,0:T(8,128)(2,1)}, u32[]{:S(2)}) copy-start(bf16[80,2,16,128]{3,2,1,0:T(8,128)(2,1)} %exchange_convolve.1.landed) | copy-start | bytes 1966084

commit v7 on v6

--- a/solution.py
+++ b/solution.py
@@ -37,7 +37,15 @@
     first_both = np.concatenate([first_high, first_low], axis=1)
     last = np.concatenate([np.cos(outer.T), -np.sin(outer.T)], axis=1) / LENGTH
     last_high, last_low = high_low(last)
-    last_all = np.concatenate([last_high, last_high, last_low], axis=1)
+    none = np.zeros_like(last_high)
+    last_all = np.block(
+        [
+            [last_high, last_high, none, none],
+            [none, none, last_high, last_high],
+            [last_low, none, none, none],
+            [none, none, last_low, none],
+        ]
+    )
     turn = 2 * np.pi * np.outer(row + 0.25, col) / LENGTH
     twist = np.stack([np.cos(turn), -np.sin(turn)]).astype(np.float32)
     inner = 2 * np.pi * (np.outer(col, col) % N2) / N2
@@ -221,27 +229,26 @@
     for half in range(2):
         wait_for(arrived.at[half], out_recv.at[half])
 
-        def unpack(n1, carry):
-            rows = arrived[half, n1].reshape(32, N2).astype(F32)
-            signals[pl.ds(pl.multiple_of(n1 * 32, 32), 32)] = rows
-            return carry
-
-        lax.fori_loop(0, N1, unpack, 0, unroll=8)
+        for n1 in range(N1):
+            signals[33 * n1 : 33 * n1 + 32] = arrived[half, n1].reshape(32, N2).astype(F32)
 
         def spectrum(index):
             block = spectra[pl.ds(pl.multiple_of(index * N1, N1), N1)]
             return block[:, :N2], block[:, N2:]
 
         def finish(indices):
-            turned = [untwisted(results[N1 * i : N1 * i + N1], twist) for i in indices]
-            high, low = split(jnp.concatenate(turned, axis=1))
-            out = dot(last_all[...], jnp.concatenate([high, low, high], axis=0))
-            return out[:, :N2], out[:, N2:]
+            data = []
+            for pair in (indices[:2], indices[2:]):
+                turned = [untwisted(results[N1 * i : N1 * i + N1], twist) for i in pair]
+                data += split(jnp.concatenate(turned, axis=1))
+            out = dot(last_all[...], jnp.concatenate(data, axis=0))
+            out = out[: 2 * N1] + out[2 * N1 :]
+            return out[:N1, :N2], out[:N1, N2:], out[N1:, :N2], out[N1:, N2:]
 
         def taps_work(group, carry):
             forward = []
             for item in range(GROUP):
-                rows = [signals[pl.ds(group * GROUP + item + HALF * i, N1, stride=32)] for i in range(2)]
+                rows = [signals[pl.ds(group * GROUP + item + HALF * i, N1, stride=33)] for i in range(2)]
                 data = jnp.concatenate(rows, axis=1).astype(BF16)
                 out = dot(first_both[...], jnp.concatenate([data, data], axis=0))
                 forward += [twisted(out[:, :N2], twist), twisted(out[:, N2:], twist)]
@@ -253,11 +260,10 @@
                 m_re, m_im = spectrum(2 * (group * GROUP + item) + 1)
                 inverse.append(jnp.concatenate([m_re * u_re + m_im * u_im, m_im * u_re - m_re * u_im], axis=1))
             results[: GROUP * N1] = middle(jnp.concatenate(inverse, axis=0), mats.at[1])
-            for item in range(0, GROUP, 2):
+            for item in range(0, GROUP, 4):
                 c = group * GROUP + item
-                first, second = finish((item, item + 1))
-                sums[half, pl.ds(c, N1, stride=HALF)] = first * scale
-                sums[half, pl.ds(c + 1, N1, stride=HALF)] = second * scale
+                for i, rows in enumerate(finish((item, item + 1, item + 2, item + 3))):
+                    sums[half, pl.ds(c + i, N1, stride=HALF)] = rows * scale
             return carry
 
         lax.fori_loop(0, HALF // GROUP, taps_work, 0)
@@ -277,26 +283,25 @@
                 inverse.append(jnp.concatenate([h_re * u_re - h_im * u_im, h_re * u_im + h_im * u_re], axis=1))
                 inverse.append(jnp.concatenate([m_re * h_re + m_im * h_im, m_im * h_re - m_re * h_im], axis=1))
             results[...] = middle(jnp.concatenate(inverse, axis=0), mats.at[1])
-            for item in range(GROUP):
+            for item in range(0, GROUP, 2):
                 c = group * GROUP + item
-                conv, inner = finish((2 * item, 2 * item + 1))
-                signals[pl.ds(c, N1, stride=32)] = conv
-                signals[pl.ds(c + HALF, N1, stride=32)] = inner
+                done = finish((2 * item, 2 * item + 1, 2 * item + 2, 2 * item + 3))
+                for i in range(2):
+                    signals[pl.ds(c + i, N1, stride=33)] = done[2 * i]
+                    signals[pl.ds(c + i + HALF, N1, stride=33)] = done[2 * i + 1]
             return carry
 
         lax.fori_loop(0, HALF // GROUP, work, 0)
 
-        def pack(n1, carry):
-            rows = signals[pl.ds(pl.multiple_of(n1 * 32, 32), 32)].astype(BF16)
-            back[half, n1] = rows.reshape(2, 16, N2)
-            return carry
-
-        lax.fori_loop(0, N1, pack, 0, unroll=8)
-        for there in partners:
+        for n1 in range(N1):
+            back[half, n1] = signals[33 * n1 : 33 * n1 + 32].astype(BF16).reshape(2, 16, N2)
+        for there in partners[:20]:
+            back_copy(half, there).start()
+        if half == 1:
+            sum_parts(half)
+        for there in partners[20:]:
             back_copy(half, there).start()
         keep[half].start()
-        if half == 1:
-            sum_parts(half)
 
     for half in range(2):
         wait_for(packed.at[half, pl.ds(0, N1 - 1)], out_send.at[half])
@@ -344,13 +349,13 @@
             pltpu.VMEM((4, rows, query.shape[1]), BF16),
             pltpu.VMEM((2 * HALF, LENGTH), F32),
             pltpu.VMEM((2 * N1, 2 * N1), BF16),
-            pltpu.VMEM((N1, 6 * N1), BF16),
+            pltpu.VMEM((4 * N1, 8 * N1), BF16),
             pltpu.VMEM((2, N1, N2), F32),
             pltpu.VMEM((2, 6 * N2, 2 * N2), BF16),
             pltpu.VMEM(slabs, BF16),
             pltpu.VMEM(slabs, BF16),
             pltpu.VMEM(slabs, BF16),
-            pltpu.VMEM((N1 * 2 * HALF, N2), F32),
+            pltpu.VMEM((N1 * (2 * HALF + 1), N2), F32),
             pltpu.VMEM((N1 * 2 * HALF, N2), F32),
             pltpu.VMEM((2 * HALF * N1, 2 * N2), F32),
             pltpu.VMEM((2 * HALF * N1, 2 * N2), F32),

time: 33.5 us -> 32.8 us (0.979)
  Pallas kernels: 31.2 us -> 30.4 us
    pallas_call x1, Pallas kernels: 30.1 us -> 29.3 us  [on_device(): pl.pallas_call(functools.partial(fused_kernel, scale), out_shape=jax.Shap...]
where the time goes in v7:
time: 32.8 us; the launch traced here: 32.2 us
  Pallas kernels  30.4 us (93%)
  local copies, waits for them, and re-layouts  1.1 us (3%)
  between operations  0.71 us (2%)
    pallas_call x1, Pallas kernels, on_device(): pl.pallas_call(functools.partial(fused_kernel, scale), out_shape=jax.Shap...  29.3 us
    pallas_call x1, Pallas kernels, on_device(): pl.pallas_call(gate_kernel, out_shape=(flat, flat, flat, jax.ShapeDtypeSt...  1.15 us
    unnamed x10, local copies, waits for them, and re-layouts  1.1 us

profile of v7, /device:TPU:1, one launch (start us, length us, event | category | flops | bytes accessed | tf_op | source)
XLA Modules:
  0.0 32.2 jit_solution(11769418036337106792)
XLA Ops:
  0.6 0.0 copy-start.1
  0.6 0.0 copy-start.2
  0.7 0.0 copy-start.3
  0.7 0.0 copy-start.4
  0.7 29.3 %exchange_convolve.1.landed = bf16[80,2,16,128]{3,2,1,0:T(8,128)(2,1)} custom-call(bf16[128,1024]{1,0:T(8,128)(2,1)} %bitcast.9, bf16[128,1024]{1,0:T(8,128)(2,1)} %bitcast.11, bf16[128,1024]{1,0:T(8,128)(2,1)} %bitcast.13, bf16[128,1024]{1,0:T(8,128)(2,1)} %bitcast.15, f32[32,4096]{1,0:T(8,128)} %bitcast.17, bf16[64,64]{1,0:T(8,128)(2,1)} %constant.8.clone.first_hbm, ...), custom_call_target="tpu_custom_call" | custom-call | tf_op jit(solution)/shard_map/exchange_convolve/pallas_call | solution.py:343
  29.9 0.0 copy-done.1
  29.9 0.0 copy-done.2
  30.0 0.0 copy-done.3
  30.0 0.0 copy-done.4
  30.0 0.0 copy-start
  30.0 1.1 %copy-done = bf16[80,2,16,128]{3,2,1,0:T(8,128)(2,1)S(1)} copy-done((bf16[80,2,16,128]{3,2,1,0:T(8,128)(2,1)S(1)}, bf16[80,2,16,128]{3,2,1,0:T(8,128)(2,1)}, u32[]{:S(2)}) %copy-start) | copy-done | bytes 655384
  31.1 1.2 %gate.1 = (bf16[128,1024]{1,0:T(8,128)(2,1)}, bf16[128,1024]{1,0:T(8,128)(2,1)}, bf16[128,1024]{1,0:T(8,128)(2,1)}, f32[32,512]{1,0:T(8,128)}) custom-call(bf16[80,2,16,128]{3,2,1,0:T(8,128)(2,1)S(1)} %copy-done, bf16[128,1024]{1,0:T(8,128)(2,1)S(1)} %bitcast.10, bf16[128,1024]{1,0:T(8,128)(2,1)S(1)} %bitcast.12, bf16[128,1024]{1,0:T(8,128)(2,1)S(1)} %bitcast.14, ...), custom_call_target="tpu_custom_call" | custom-call | tf_op jit(solution)/shard_map/gate/pallas_call | solution.py:381
Async XLA Ops:
  0.6 29.3 %copy-start.1 = (bf16[1,128,1024]{2,1,0:T(8,128)(2,1)S(1)}, bf16[1,128,1024]{2,1,0:T(8,128)(2,1)}, u32[]{:S(2)}) copy-start(bf16[1,128,1024]{2,1,0:T(8,128)(2,1)} %param.9) | copy-start | bytes 786436
  0.6 29.3 %copy-start.2 = (bf16[1,128,1024]{2,1,0:T(8,128)(2,1)S(1)}, bf16[1,128,1024]{2,1,0:T(8,128)(2,1)}, u32[]{:S(2)}) copy-start(bf16[1,128,1024]{2,1,0:T(8,128)(2,1)} %param.10) | copy-start | bytes 786436
  0.7 29.3 %copy-start.3 = (bf16[1,128,1024]{2,1,0:T(8,128)(2,1)S(1)}, bf16[1,128,1024]{2,1,0:T(8,128)(2,1)}, u32[]{:S(2)}) copy-start(bf16[1,128,1024]{2,1,0:T(8,128)(2,1)} %param.11) | copy-start | bytes 786436
  0.7 29.3 %copy-start.4 = (bf16[1,128,1024]{2,1,0:T(8,128)(2,1)S(1)}, bf16[1,128,1024]{2,1,0:T(8,128)(2,1)}, u32[]{:S(2)}) copy-start(bf16[1,128,1024]{2,1,0:T(8,128)(2,1)} %param.12) | copy-start | bytes 786436
  30.0 1.1 %copy-start = (bf16[80,2,16,128]{3,2,1,0:T(8,128)(2,1)S(1)}, bf16[80,2,16,128]{3,2,1,0:T(8,128)(2,1)}, u32[]{:S(2)}) copy-start(bf16[80,2,16,128]{3,2,1,0:T(8,128)(2,1)} %exchange_convolve.1.landed) | copy-start | bytes 1966084
